TPU v7x, 128 devices: a whole 4x4x4 slice. The times are simulated.
128 devices in a mesh: seq: 16 (over x_lo, y, core), head: 8 (over z, x_hi).
Axes of the slice: x: 4 (x_hi: 2, x_lo: 2; x = x_hi * 2 + x_lo), y: 4, z: 4, core: 2. Of those that a mesh axis runs over, the one named last changes fastest.
Arguments:
- out_grad: bfloat16 [16384, 6144], P(('seq', 'head')), may hold values from -96 to 96
- expert_rows: bfloat16 [8, 8192, 6144], P('head', 'seq'), may hold values from -96 to 96
- expert_ids: int32 [16384, 2], P(('seq', 'head')), may hold values from 0 to 7, all different within a row; in each aligned block of 128 rows (0 to 127, 128 to 255, ...) at most 64 rows name the same one
- gates: float32 [16384, 2], P(('seq', 'head')), may hold values from 0.1 to 0.9
- out_proj: bfloat16 [3072, 6144], P('head'), may hold values from -0.078125 to 0.078125
- attention_output: bfloat16 [24, 16384, 128], P('head', 'seq'), may hold values from -0.0029296875 to 0.0029296875
- saved_queries: bfloat16 [24, 16384, 128], P('head', 'seq'), may hold values from -1.6953125 to 1.6953125
- saved_keys: bfloat16 [8, 16384, 128], P('head', 'seq'), may hold values from -1.6953125 to 1.6953125
- saved_values: bfloat16 [8, 16384, 128], P('head', 'seq'), may hold values from -6 to 6
- softmax_normalizer: float32 [24, 16384], P('head', 'seq'), may hold values from 8 to 9.5
Outputs:
- grad_query: bfloat16 [16384, 3072], P(('seq', 'head'))
- key_gradient_rows: bfloat16 [16384, 1024], P(('seq', 'head'))
- value_gradient_rows: bfloat16 [16384, 1024], P(('seq', 'head'))
- grad_proj: bfloat16 [3072, 6144], P('head')
Inputs may be any that keep to these rules, and one draw needn't show every extreme that they name: `expert_ids`: each row names 2 different experts. In each aligned block of 128 rows (the tokens of one device) no expert is named more than 64 times, a bound that some block reaches.
All inputs are finite; a program needn't handle non-finite values.
Results may differ from a plain program's by a relative error of at most 0.0065.
Values may be sent and summed in bfloat16 or wider, within the bound.
A program may use at most 128 MiB of HBM per device.

v0:
```python
import math

import jax
import jax.numpy as jnp
from jax import lax
from jax.sharding import PartitionSpec as P

WIN = 4096


def shifted(block, axis, distance):
    devices = range(lax.axis_size(axis))
    route = [(i - distance, i) for i in devices if i - distance in devices]
    return lax.ppermute(block, axis, route)


def routed_rows(returned, expert_ids):
    experts = returned.shape[0]
    capacity = returned.shape[1]
    model_width = returned.shape[2]
    pair_ids = expert_ids.reshape(-1)
    onehot = (pair_ids[:, None] == jnp.arange(experts, dtype=jnp.int32)[None, :]).astype(jnp.int32)
    before = jnp.cumsum(onehot, axis=0) - onehot
    slot_rank = jnp.sum(before * onehot, axis=1)
    flat_index = pair_ids * capacity + slot_rank
    row_table = returned.reshape(experts * capacity, model_width)
    picked = jnp.take(row_table, flat_index, axis=0)
    return picked.reshape(expert_ids.shape[0], expert_ids.shape[1], model_width)


def local(
    out_grad,
    expert_rows,
    expert_ids,
    gates,
    out_proj,
    attention_output,
    saved_queries,
    saved_keys,
    saved_values,
    softmax_normalizer,
):
    heads_dev, seq_dev, head_dim = saved_queries.shape
    kv_dev = saved_keys.shape[0]
    group_size = heads_dev // kv_dev
    model_width = out_grad.shape[1]
    returned = lax.all_to_all(expert_rows, "head", split_axis=1, concat_axis=0, tiled=True)
    picked = routed_rows(returned, expert_ids)
    summed = out_grad.astype(jnp.float32)
    summed = summed + gates[:, 0:1] * picked[:, 0].astype(jnp.float32)
    summed = summed + gates[:, 1:2] * picked[:, 1].astype(jnp.float32)
    hidden = summed.astype(jnp.bfloat16)
    piece = lax.all_gather(hidden, "head", axis=0, tiled=True)
    fresh_rows = lax.dot_general(
        piece, out_proj, (((1,), (1,)), ((), ())), preferred_element_type=jnp.float32
    ).astype(jnp.bfloat16)
    partial_value = lax.dot_general(
        attention_output, piece, (((1,), (0,)), ((), ())), preferred_element_type=jnp.float32
    )
    grad_out, partial_value = (fresh_rows, partial_value)
    summed_proj = lax.psum(partial_value, "seq")
    grad_proj = summed_proj.astype(jnp.bfloat16).reshape(heads_dev * head_dim, model_width)
    head_gradients = jnp.transpose(grad_out.reshape(seq_dev, heads_dev, head_dim), (1, 0, 2))
    row_delta = jnp.sum(
        head_gradients.astype(jnp.float32) * attention_output.astype(jnp.float32), axis=2
    )
    window = WIN
    span_count = (window + seq_dev - 1) // seq_dev
    offset = span_count * seq_dev
    kv_pair = jnp.stack([saved_keys, saved_values], axis=0)
    earlier = []
    for distance in range(span_count, 0, -1):
        earlier.append(shifted(kv_pair, "seq", distance))
    extended = jnp.concatenate(earlier + [kv_pair], axis=2)
    block_rows = min(512, seq_dev)
    key_span = window + block_rows
    score_scale = 1.0 / math.sqrt(head_dim)
    seq_pos = lax.axis_index("seq")
    rows_iota = lax.broadcasted_iota(jnp.int32, (block_rows, key_span), 0)
    cols_iota = lax.broadcasted_iota(jnp.int32, (block_rows, key_span), 1)
    in_band = (cols_iota >= rows_iota + 1) & (cols_iota <= rows_iota + window)
    ext_len = offset + seq_dev

    def block_step(index, carry):
        dk_ext, dv_ext, dq_all = carry
        first_row = index * block_rows
        key_start = first_row + (offset - window)
        usable = in_band & (cols_iota + key_start >= offset - seq_pos * seq_dev)
        key_blk = lax.dynamic_slice_in_dim(extended[0, 0], key_start, key_span, 0)
        value_blk = lax.dynamic_slice_in_dim(extended[1, 0], key_start, key_span, 0)
        dk_blk = jnp.zeros((key_span, head_dim), jnp.float32)
        dv_blk = jnp.zeros((key_span, head_dim), jnp.float32)
        for q_head in range(0, group_size):
            query_blk = lax.dynamic_slice_in_dim(saved_queries[q_head], first_row, block_rows, 0)
            grad_blk = lax.dynamic_slice(
                grad_out, (first_row, q_head * head_dim), (block_rows, head_dim)
            )
            lse_blk = lax.dynamic_slice_in_dim(softmax_normalizer[q_head], first_row, block_rows, 0)
            delta_blk = lax.dynamic_slice_in_dim(row_delta[q_head], first_row, block_rows, 0)
            scores = (
                lax.dot_general(
                    query_blk, key_blk, (((1,), (1,)), ((), ())), preferred_element_type=jnp.float32
                )
                * score_scale
            )
            probability = jnp.where(usable, jnp.exp(scores - lse_blk[:, None]), 0.0)
            grad_prob = lax.dot_general(
                grad_blk, value_blk, (((1,), (1,)), ((), ())), preferred_element_type=jnp.float32
            )
            grad_score = probability * (grad_prob - delta_blk[:, None])
            prob_half = probability.astype(jnp.bfloat16)
            score_half = grad_score.astype(jnp.bfloat16)
            dv_blk = dv_blk + lax.dot_general(
                prob_half, grad_blk, (((0,), (0,)), ((), ())), preferred_element_type=jnp.float32
            )
            dk_blk = dk_blk + score_scale * lax.dot_general(
                score_half, query_blk, (((0,), (0,)), ((), ())), preferred_element_type=jnp.float32
            )
            dq_blk = score_scale * jnp.dot(score_half, key_blk, preferred_element_type=jnp.float32)
            dq_all = lax.dynamic_update_slice(dq_all, dq_blk, (first_row, q_head * head_dim))
        old_key = lax.dynamic_slice(dk_ext, (0, key_start, 0), (1, key_span, head_dim))
        dk_ext = lax.dynamic_update_slice(dk_ext, old_key + dk_blk[None], (0, key_start, 0))
        old_value = lax.dynamic_slice(dv_ext, (0, key_start, 0), (1, key_span, head_dim))
        dv_ext = lax.dynamic_update_slice(dv_ext, old_value + dv_blk[None], (0, key_start, 0))
        return (dk_ext, dv_ext, dq_all)

    loop_carry = (
        jnp.zeros((kv_dev, ext_len, head_dim), jnp.float32),
        jnp.zeros((kv_dev, ext_len, head_dim), jnp.float32),
        jnp.zeros((seq_dev, heads_dev * head_dim), jnp.float32),
    )
    dk_ext, dv_ext, dq_all = lax.fori_loop(0, seq_dev // block_rows, block_step, loop_carry)
    grads_ext = jnp.stack([dk_ext, dv_ext], axis=0)
    total_kv = grads_ext[:, :, offset:, :]
    for distance in range(1, span_count + 1):
        far_part = grads_ext[
            :, :, offset - distance * seq_dev : offset - (distance - 1) * seq_dev, :
        ]
        total_kv = total_kv + shifted(far_part, "seq", -distance)
    kv_half = total_kv.astype(jnp.bfloat16)
    dk_cols = jnp.transpose(kv_half[0], (1, 0, 2)).reshape(seq_dev, kv_dev * head_dim)
    dv_cols = jnp.transpose(kv_half[1], (1, 0, 2)).reshape(seq_dev, kv_dev * head_dim)
    dq_cols = dq_all.astype(jnp.bfloat16)
    grad_query, key_gradient_rows, value_gradient_rows = (
        lax.all_to_all(dq_cols, "head", split_axis=0, concat_axis=1, tiled=True),
        lax.all_to_all(dk_cols, "head", split_axis=0, concat_axis=1, tiled=True),
        lax.all_to_all(dv_cols, "head", split_axis=0, concat_axis=1, tiled=True),
    )
    return (grad_query, key_gradient_rows, value_gradient_rows, grad_proj)


def solution(mesh):
    in_specs = (
        P(("seq", "head"), None),
        P("head", "seq", None),
        P(("seq", "head"), None),
        P(("seq", "head"), None),
        P("head", None),
        P("head", "seq", None),
        P("head", "seq", None),
        P("head", "seq", None),
        P("head", "seq", None),
        P("head", "seq"),
    )
    out_specs = (
        P(("seq", "head"), None),
        P(("seq", "head"), None),
        P(("seq", "head"), None),
        P("head", None),
    )
    return jax.shard_map(local, mesh=mesh, in_specs=in_specs, out_specs=out_specs, check_vma=False)
```

profile of v0, /device:TPU:24, one launch (start us, length us, event | category | flops | bytes accessed | tf_op | source)
XLA Modules:
  0.0 756.6 jit_solution(4666393536093147817)
XLA Ops:
  7.2 12.2 %copy.78 = bf16[1,512,6144]{2,0,1:T(2,128)(2,1)} copy(bf16[1,512,6144]{2,1,0:T(8,128)(2,1)} %param.13) | data formatting | bytes 12582912 | tf_op args[1]
  19.9 38.9 %reduce.2 = bf16[512,6144]{1,0:T(8,128)(2,1)} reduce(bf16[512,1,6144]{2,1,0:T(2,128)(2,1)} %bitcast.199, bf16[]{:T(256)} %broadcast.111), dimensions={1}, to_apply=%bitcast.134.reduce_sub_computation | reduce | bytes 12582914
  58.8 9.4 %reshape.158 = bf16[8,2,196608]{2,1,0:T(2,128)(2,1)} reshape(bf16[512,6144]{1,0:T(8,128)(2,1)} %reduce.2) | data formatting | bytes 12582912
  68.2 7.9 %all-to-all-start = ((bf16[8,2,196608]{2,1,0:T(2,128)(2,1)}), bf16[8,2,196608]{2,1,0:T(2,128)(2,1)}, u32[]{:S(2)}, u32[]{:S(2)}) async-start(bf16[8,2,196608]{2,1,0:T(2,128)(2,1)} %reshape.158), calls=%async_computation | async-start | bytes 12582912 | tf_op jit(solution)/shard_map/all_to_all | solution.py:47
  79.8 69.8 %all-to-all-done = bf16[8,2,196608]{2,1,0:T(2,128)(2,1)} async-done(((bf16[8,2,196608]{2,1,0:T(2,128)(2,1)}), bf16[8,2,196608]{2,1,0:T(2,128)(2,1)}, u32[]{:S(2)}, u32[]{:S(2)}) %all-to-all-start) | async-done | bytes 6291488 | tf_op jit(solution)/shard_map/all_to_all | solution.py:47
  149.6 11.0 %reshape.159 = bf16[512,1,6144]{2,1,0:T(2,128)(2,1)} reshape(bf16[8,2,196608]{2,1,0:T(2,128)(2,1)} %all-to-all-done) | data formatting | bytes 12582912
  160.6 11.0 %copy.77 = bf16[1,512,6144]{2,1,0:T(8,128)(2,1)} copy(bf16[1,512,6144]{2,0,1:T(2,128)(2,1)} %bitcast.198) | data formatting | bytes 12582912
  171.6 9.1 %gather_fusion = bf16[256,6144]{1,0:T(8,128)(2,1)S(1)} fusion(bf16[512,6144]{1,0:T(8,128)(2,1)} %bitcast.197, s32[1024]{0:T(1024)S(1)} %pad_clamp_fusion), kind=kCustom, calls=%fused_computation | custom fusion | bytes 6292480 | tf_op jit(solution)/shard_map/jit(_take)/gather | solution.py:27
  183.9 7.7 %copy.64 = bf16[128,2,6144]{0,2,1:T(8,128)(2,1)S(1)} copy(bf16[128,2,6144]{2,1,0:T(2,128)(2,1)} %gather.7) | data formatting | bytes 6291456 | tf_op jit(solution)/shard_map/jit(_take)/gather | solution.py:27
  201.1 4.0 collective-permute-start.2
  207.2 12.0 %collective-permute-done = bf16[2,1,1024,128]{3,2,1,0:T(8,128)(2,1)} collective-permute-done((bf16[2,1,1024,128]{3,2,1,0:T(8,128)(2,1)}, bf16[2,1,1024,128]{3,2,1,0:T(8,128)(2,1)}, u32[]{:S(2)}, u32[]{:S(2)}) %collective-permute-start) | collective-permute-done | bytes 524320 | tf_op jit(solution)/shard_map/ppermute | solution.py:14
  220.3 19.5 %collective-permute-done.1 = bf16[2,1,1024,128]{3,2,1,0:T(8,128)(2,1)} collective-permute-done((bf16[2,1,1024,128]{3,2,1,0:T(8,128)(2,1)}, bf16[2,1,1024,128]{3,2,1,0:T(8,128)(2,1)}, u32[]{:S(2)}, u32[]{:S(2)}) %collective-permute-start.1) | collective-permute-done | bytes 524320 | tf_op jit(solution)/shard_map/ppermute | solution.py:14
  240.9 10.1 %collective-permute-done.2 = bf16[2,1,1024,128]{3,2,1,0:T(8,128)(2,1)} collective-permute-done((bf16[2,1,1024,128]{3,2,1,0:T(8,128)(2,1)}, bf16[2,1,1024,128]{3,2,1,0:T(8,128)(2,1)}, u32[]{:S(2)}, u32[]{:S(2)}) %collective-permute-start.2) | collective-permute-done | bytes 524320 | tf_op jit(solution)/shard_map/ppermute | solution.py:14
  253.4 108.9 %all-gather.2.cloned.1.call-done = bf16[1024,6144]{0,1:T(8,128)(2,1)} async-done(((bf16[128,6144]{0,1:T(8,128)(2,1)}), bf16[1024,6144]{0,1:T(8,128)(2,1)}) %all-gather.2.cloned.1.call-update) | async-done | bytes 12582928 | tf_op jit(solution)/shard_map/all_gather | solution.py:53
  362.2 10.1 %convolution_convert_fusion = bf16[1024,384]{0,1:T(8,128)(2,1)} fusion(bf16[384,6144]{1,0:T(8,128)(2,1)} %param.16, bf16[1024,6144]{0,1:T(8,128)(2,1)} %all-gather.2.cloned.1.call-done), kind=kOutput, calls=%fused_computation.121 | convolution fusion | flops 4832231424 | bytes 18087936 | tf_op jit(solution)/shard_map/dot_general | solution.py:54
  382.8 99.3 %while.20 = (s32[]{:T(128)}, f32[1,5120,128]{2,1,0:T(8,128)}, f32[1,5120,128]{2,1,0:T(8,128)}, bf16[1024,384]{1,0:T(8,128)(2,1)}, s32[]{:T(128)}, /*index=5*/bf1...) while((s32[]{:T(128)}, f32[1,5120,128]{2,1,0:T(8,128)}, ...), condition=%wide.region_5.6_spmd.clone, body=%wide.region_4.5_spmd.clone.sunk | while | flops 9156034560 | bytes 252151056 | solution.py:132
  385.8 3.8 exponential_select_fusion.8
  393.3 3.8 exponential_select_fusion.7
  400.8 5.2 exponential_select_fusion.6
  410.7 4.9 fusion.204
  427.7 4.7 fusion.202
  450.3 5.2 exponential_select_fusion.6
  460.2 4.9 fusion.204
  477.2 4.7 fusion.202
  482.1 3.9 fusion.109
  498.7 10.7 %collective-permute-done.4 = f32[2,1,1024,128]{3,2,1,0:T(8,128)S(1)} collective-permute-done((f32[2,1,1024,128]{3,2,1,0:T(8,128)}, f32[2,1,1024,128]{3,2,1,0:T(8,128)S(1)}, u32[]{:S(2)}, u32[]{:S(2)}) %collective-permute-start.4) | collective-permute-done | bytes 1048608 | tf_op jit(solution)/shard_map/ppermute | solution.py:14
  509.4 50.9 %collective-permute-done.5 = f32[2,1,1024,128]{3,2,1,0:T(8,128)} collective-permute-done((f32[2,1,1024,128]{3,2,1,0:T(8,128)}, f32[2,1,1024,128]{3,2,1,0:T(8,128)}, u32[]{:S(2)}, u32[]{:S(2)}) %collective-permute-start.5) | collective-permute-done | bytes 1048608 | tf_op jit(solution)/shard_map/ppermute | solution.py:14
  560.3 27.1 %collective-permute-done.6 = f32[2,1,1024,128]{3,2,1,0:T(8,128)} collective-permute-done((f32[2,1,1024,128]{3,2,1,0:T(8,128)S(1)}, f32[2,1,1024,128]{3,2,1,0:T(8,128)}, u32[]{:S(2)}, u32[]{:S(2)}) %collective-permute-start.6) | collective-permute-done | bytes 1048608 | tf_op jit(solution)/shard_map/ppermute | solution.py:14
  594.1 11.8 %fusion.95 = f32[3,128,6144]{1,2,0:T(8,128)} fusion(bf16[3,1024,128]{2,1,0:T(8,128)(2,1)S(1)} %copy-done.16, bf16[1024,6144]{0,1:T(8,128)(2,1)} %all-gather.2.cloned.1.call-done), kind=kOutput, calls=%fused_computation.101 | convolution fusion | flops 4831838208 | bytes 22806528 | tf_op jit(solution)/shard_map/dot_general | solution.py:57
  606.0 7.1 all-to-all-start.3
  613.1 126.0 %all-reduce.1 = bf16[3,128,6144]{1,2,0:T(8,128)(2,1)} all-reduce(f32[3,128,6144]{1,2,0:T(8,128)} %fusion.95), channel_id=1, replica_groups=mesh['seq'=16,'head'=8] {'seq'}, use_global_device_ids=true, to_apply=%region_6.7 | all-reduce | flops 2359296 | bytes 14155776 | tf_op jit(solution)/shard_map/psum | solution.py:61
  739.1 6.6 copy.70
  (184 shorter events, 118.1 us)
Async XLA Ops:
  68.2 8.0 %copy-start.18 = (s32[128,2]{0,1:T(2,128)S(1)}, s32[128,2]{0,1:T(2,128)}, u32[]{:S(2)}) copy-start(s32[128,2]{0,1:T(2,128)} %param.14) | copy-start | bytes 3076
  68.2 10.0 %copy-start.13 = (bf16[128,6144]{1,0:T(8,128)(2,1)S(1)}, bf16[128,6144]{1,0:T(8,128)(2,1)}, u32[]{:S(2)}) copy-start(bf16[128,6144]{1,0:T(8,128)(2,1)} %param.12) | copy-start | bytes 4718596
  68.2 81.4 %all-to-all-start = ((bf16[8,2,196608]{2,1,0:T(2,128)(2,1)}), bf16[8,2,196608]{2,1,0:T(2,128)(2,1)}, u32[]{:S(2)}, u32[]{:S(2)}) async-start(bf16[8,2,196608]{2,1,0:T(2,128)(2,1)} %reshape.158), calls=%async_computation | async-start | bytes 12582912 | tf_op jit(solution)/shard_map/all_to_all | solution.py:47
  76.1 286.1 %all-gather.2.cloned.1.call-start = ((), (), s32[]{:S(2)}) async-start(), calls=%async_computation.4 | async-start | bytes 14155776 | tf_op jit(solution)/shard_map/all_gather | solution.py:53
  195.9 23.4 %collective-permute-start = (bf16[2,1,1024,128]{3,2,1,0:T(8,128)(2,1)}, bf16[2,1,1024,128]{3,2,1,0:T(8,128)(2,1)}, u32[]{:S(2)}, u32[]{:S(2)}) collective-permute-start(bf16[2,1,1024,128]{3,2,1,0:T(8,128)(2,1)} %pad_maximum_fusion.1), channel_id=1, source_target_pairs={{0,32},{8,40},{16,48},{24,56},{32,64},{40,72},{48,80},{56,88},{64,... | collective-permute-start | bytes 1572872 | tf_op jit(solution)/shard_map/ppermute | solution.py:14
  199.0 40.8 %collective-permute-start.1 = (bf16[2,1,1024,128]{3,2,1,0:T(8,128)(2,1)}, bf16[2,1,1024,128]{3,2,1,0:T(8,128)(2,1)}, u32[]{:S(2)}, u32[]{:S(2)}) collective-permute-start(bf16[2,1,1024,128]{3,2,1,0:T(8,128)(2,1)} %pad_maximum_fusion.1), channel_id=1, source_target_pairs={{0,24},{8,32},{16,40},{24,48},{32,56},{40,64},{48,72},{56,80},{64,... | collective-permute-start | bytes 1572872 | tf_op jit(solution)/shard_map/ppermute | solution.py:14
  201.1 50.0 %collective-permute-start.2 = (bf16[2,1,1024,128]{3,2,1,0:T(8,128)(2,1)}, bf16[2,1,1024,128]{3,2,1,0:T(8,128)(2,1)}, u32[]{:S(2)}, u32[]{:S(2)}) collective-permute-start(bf16[2,1,1024,128]{3,2,1,0:T(8,128)(2,1)} %pad_maximum_fusion.1), channel_id=1, source_target_pairs={{0,16},{8,24},{16,32},{24,40},{32,48},{40,56},{48,64},{56,72},{64,... | collective-permute-start | bytes 1572872 | tf_op jit(solution)/shard_map/ppermute | solution.py:14
  205.1 47.1 %collective-permute-start.3 = (bf16[2,1,1024,128]{3,2,1,0:T(8,128)(2,1)}, bf16[2,1,1024,128]{3,2,1,0:T(8,128)(2,1)}, u32[]{:S(2)}, u32[]{:S(2)}) collective-permute-start(bf16[2,1,1024,128]{3,2,1,0:T(8,128)(2,1)} %pad_maximum_fusion.1), channel_id=1, source_target_pairs={{0,8},{8,16},{16,24},{24,32},{32,40},{40,48},{48,56},{56,64},{64,7... | collective-permute-start | bytes 1572872 | tf_op jit(solution)/shard_map/ppermute | solution.py:14
  383.0 14.1 %copy-start.5 = (bf16[1024,384]{1,0:T(8,128)(2,1)}, bf16[1024,384]{1,0:T(8,128)(2,1)S(1)}, u32[]{:S(2)}) copy-start(bf16[1024,384]{1,0:T(8,128)(2,1)S(1)} %get-tuple-element.567) | copy-start | bytes 2359300 | tf_op jit(solution)/shard_map/while
  385.6 7.6 %copy-start.9 = (bf16[1,1024,128]{2,1,0:T(8,128)(2,1)}, bf16[1,1024,128]{2,1,0:T(8,128)(2,1)S(1)}, u32[]{:S(2)}) copy-start(bf16[1,1024,128]{2,1,0:T(8,128)(2,1)S(1)} %get-tuple-element.520) | copy-start | bytes 786436 | tf_op jit(solution)/shard_map/while
  385.8 7.5 copy-start.3
  385.8 11.3 %copy-start = (bf16[1,1,5120,128]{3,2,1,0:T(8,128)(2,1)}, bf16[1,1,5120,128]{3,2,1,0:T(8,128)(2,1)S(1)}, u32[]{:S(2)}) copy-start(bf16[1,1,5120,128]{3,2,1,0:T(8,128)(2,1)S(1)} %get-tuple-element.518) | copy-start | bytes 3932164 | tf_op jit(solution)/shard_map/while
  410.7 11.4 %slice-start.2 = ((s8[4718592]{0:T(1024)(128)(4,1)}), s8[4194304]{0:T(1024)(128)(4,1)S(1)}, s32[]{:S(2)}) async-start(s8[4718592]{0:T(1024)(128)(4,1)} %bitcast.195), calls=%async_computation.7 | async-start | bytes 8388608 | tf_op jit(solution)/shard_map/while
  415.6 6.5 slice-start.3
  420.6 5.0 slice-start
  427.7 4.7 copy-start.2
  427.7 4.7 copy-start.6
  432.5 14.1 %copy-start.5 = (bf16[1024,384]{1,0:T(8,128)(2,1)}, bf16[1024,384]{1,0:T(8,128)(2,1)S(1)}, u32[]{:S(2)}) copy-start(bf16[1024,384]{1,0:T(8,128)(2,1)S(1)} %get-tuple-element.567) | copy-start | bytes 2359300 | tf_op jit(solution)/shard_map/while
  435.1 7.6 %copy-start.9 = (bf16[1,1024,128]{2,1,0:T(8,128)(2,1)}, bf16[1,1024,128]{2,1,0:T(8,128)(2,1)S(1)}, u32[]{:S(2)}) copy-start(bf16[1,1024,128]{2,1,0:T(8,128)(2,1)S(1)} %get-tuple-element.520) | copy-start | bytes 786436 | tf_op jit(solution)/shard_map/while
  435.3 7.5 copy-start.3
  435.3 11.3 %copy-start = (bf16[1,1,5120,128]{3,2,1,0:T(8,128)(2,1)}, bf16[1,1,5120,128]{3,2,1,0:T(8,128)(2,1)S(1)}, u32[]{:S(2)}) copy-start(bf16[1,1,5120,128]{3,2,1,0:T(8,128)(2,1)S(1)} %get-tuple-element.518) | copy-start | bytes 3932164 | tf_op jit(solution)/shard_map/while
  460.2 11.4 %slice-start.2 = ((s8[4718592]{0:T(1024)(128)(4,1)}), s8[4194304]{0:T(1024)(128)(4,1)S(1)}, s32[]{:S(2)}) async-start(s8[4718592]{0:T(1024)(128)(4,1)} %bitcast.195), calls=%async_computation.7 | async-start | bytes 8388608 | tf_op jit(solution)/shard_map/while
  465.1 6.5 slice-start.3
  470.1 5.0 slice-start
  486.0 23.4 %collective-permute-start.4 = (f32[2,1,1024,128]{3,2,1,0:T(8,128)}, f32[2,1,1024,128]{3,2,1,0:T(8,128)S(1)}, u32[]{:S(2)}, u32[]{:S(2)}) collective-permute-start(f32[2,1,1024,128]{3,2,1,0:T(8,128)} %get-tuple-element.420), channel_id=1, source_target_pairs={{8,0},{16,8},{24,16},{32,24},{40,32},{48,40},{56,48},{64,56},{72,6... | collective-permute-start | bytes 3145736 | tf_op jit(solution)/shard_map/ppermute | solution.py:14
  487.9 72.4 %collective-permute-start.5 = (f32[2,1,1024,128]{3,2,1,0:T(8,128)}, f32[2,1,1024,128]{3,2,1,0:T(8,128)}, u32[]{:S(2)}, u32[]{:S(2)}) collective-permute-start(f32[2,1,1024,128]{3,2,1,0:T(8,128)} %get-tuple-element.421), channel_id=1, source_target_pairs={{16,0},{24,8},{32,16},{40,24},{48,32},{56,40},{64,48},{72,56},{80,... | collective-permute-start | bytes 3145736 | tf_op jit(solution)/shard_map/ppermute | solution.py:14
  490.7 69.6 %collective-permute-start.7 = (f32[2,1,1024,128]{3,2,1,0:T(8,128)}, f32[2,1,1024,128]{3,2,1,0:T(8,128)}, u32[]{:S(2)}, u32[]{:S(2)}) collective-permute-start(f32[2,1,1024,128]{3,2,1,0:T(8,128)} %get-tuple-element.422), channel_id=1, source_target_pairs={{32,0},{40,8},{48,16},{56,24},{64,32},{72,40},{80,48},{88,56},{96,... | collective-permute-start | bytes 3145736 | tf_op jit(solution)/shard_map/ppermute | solution.py:14
  493.2 94.2 %collective-permute-start.6 = (f32[2,1,1024,128]{3,2,1,0:T(8,128)S(1)}, f32[2,1,1024,128]{3,2,1,0:T(8,128)}, u32[]{:S(2)}, u32[]{:S(2)}) collective-permute-start(f32[2,1,1024,128]{3,2,1,0:T(8,128)S(1)} %get-tuple-element.423), channel_id=1, source_target_pairs={{24,0},{32,8},{40,16},{48,24},{56,32},{64,40},{72,48},{80,56},{88,... | collective-permute-start | bytes 3145736 | tf_op jit(solution)/shard_map/ppermute | solution.py:14
  495.1 95.6 %all-to-all-start.1 = ((bf16[8,128,384]{2,1,0:T(8,128)(2,1)}), bf16[8,128,384]{2,1,0:T(8,128)(2,1)S(1)}, u32[]{:S(2)}, u32[]{:S(2)}) async-start(bf16[8,128,384]{2,1,0:T(8,128)(2,1)} %bitcast.12), calls=%async_computation.1 | async-start | bytes 1572864 | tf_op jit(solution)/shard_map/all_to_all | solution.py:145
  587.4 6.7 copy-start.16
  590.7 15.3 %all-to-all-start.2 = ((bf16[8,128,128]{2,1,0:T(8,128)(2,1)}), bf16[8,128,128]{2,1,0:T(8,128)(2,1)S(1)}, u32[]{:S(2)}, u32[]{:S(2)}) async-start(bf16[8,128,128]{2,1,0:T(8,128)(2,1)} %bitcast.17), calls=%async_computation.2 | async-start | bytes 524288 | tf_op jit(solution)/shard_map/all_to_all | solution.py:146
  606.0 142.4 %all-to-all-start.3 = ((bf16[8,128,128]{2,1,0:T(8,128)(2,1)}), bf16[8,128,128]{2,1,0:T(8,128)(2,1)S(1)}, u32[]{:S(2)}, u32[]{:S(2)}) async-start(bf16[8,128,128]{2,1,0:T(8,128)(2,1)} %bitcast.20), calls=%async_computation.3 | async-start | bytes 524288 | tf_op jit(solution)/shard_map/all_to_all | solution.py:147
  (21 other events, 60.6 us)
Sparse Core Ops, SparseCore 0:
  195.1 167.0 all-gather.1
where the time goes:
time: 768 us; the launch traced here: 757 us
  waiting for transfers between devices  309 us (40%)
  blocking collectives  126 us (16%)
  matrix products  115 us (15%)
  local copies, waits for them, and re-layouts  97.2 us (13%)
  other arithmetic  51.5 us (7%)
  starting transfers between devices  42.4 us (6%)
  between operations  14.7 us (2%)
    ppermute x8, waiting for transfers between devices, shifted(): return lax.ppermute(block, axis, route)  130 us
    psum x1, blocking collectives, local(): summed_proj = lax.psum(partial_value, 'seq')  126 us
    all_gather x1, waiting for transfers between devices, local(): piece = lax.all_gather(hidden, 'head', axis=0, tiled=True)  109 us
    all_to_all x1, waiting for transfers between devices, local(): lax.all_to_all(expert_rows, 'head', split_axis=1, concat_axis=0, tiled=True)  69.8 us
    unnamed x31, local copies, waits for them, and re-layouts  55.6 us
    unnamed x1, other arithmetic  38.9 us
    dot_general x6, matrix products, block_step(): lax.dot_general(query_blk, key_blk, (((1,), (1,)), ((), ())), preferred_e...  25.6 us
    dot_general x6, matrix products, block_step(): lax.dot_general(grad_blk, value_blk, (((1,), (1,)), ((), ())), preferred_...  20.5 us
  transfers between devices with their start and end apart: 13, of which 8 were waited for; matrix products, arithmetic and copies ran while one was open for 4% of the time, Pallas kernels for 0%

commit v1 on v0

v1 whole, which is shorter than its diff:
```python
import functools
import math

import jax
import jax.numpy as jnp
from jax import lax
from jax.experimental import pallas as pl
from jax.experimental.pallas import tpu as pltpu
from jax.sharding import PartitionSpec as P

WIN = 4096
LOG2E = 1.4426950408889634
MESH = pl.DeviceIdType.MESH
NZ = 4
NEAR = (((1,), (1,)), ((), ()))


def gather_kernel(
    chunks,
    rows_hbm, ids_ref, gates_ref, resid_hbm, proj_hbm, attn_ref, key_hbm, value_hbm,
    gout_ref, gproj_ref, kx_hbm, vx_hbm,
    recv, hid, proj, attn_t, resid, pick, acc,
    a2a_send, a2a_recv, ag_send, ag_recv, kv_send, kv_recv, loc,
):
    seq = lax.axis_index("seq")
    me = lax.axis_index("head")
    n_seq = lax.axis_size("seq")
    z, x = me // 2, lax.rem(me, 2)
    heads = 2 * NZ
    tok, width = resid.shape
    cap = recv.shape[0] // heads
    w = width // chunks
    piece = w // 4
    span = kx_hbm.shape[0] // key_hbm.shape[0] - 1
    seq_dev = key_hbm.shape[0]

    def at(dz, flip):
        return lax.rem(z + dz, NZ) * 2 + (lax.rem(x + 1, 2) if flip else x)

    barrier = pltpu.get_barrier_semaphore()
    for d in range(1, heads):
        pl.semaphore_signal(barrier, inc=1, device_id=(seq, lax.rem(me + d, heads)), device_id_type=MESH)
    for d in range(1, span + 1):
        @pl.when(seq >= d)
        def _():
            pl.semaphore_signal(barrier, inc=1, device_id=(seq - d, me), device_id_type=MESH)
    pl.semaphore_wait(barrier, heads - 1 + jnp.minimum(span, n_seq - 1 - seq))

    def a2a(c, d):
        peer = lax.rem(me + d, heads)
        return pltpu.make_async_remote_copy(
            src_ref=rows_hbm.at[pl.ds(pl.multiple_of(peer * cap, cap), cap), pl.ds(c * w, w)],
            dst_ref=recv.at[pl.ds(pl.multiple_of(me * cap, cap), cap), pl.ds(c * w, w)],
            send_sem=a2a_send.at[c, d - 1],
            recv_sem=a2a_recv.at[c, d - 1],
            device_id=(seq, peer),
            device_id_type=MESH,
        )

    own = pl.ds(pl.multiple_of(me * cap, cap), cap)
    local = [
        pltpu.make_async_copy(rows_hbm.at[own, :], recv.at[own, :], loc.at[0]),
        pltpu.make_async_copy(resid_hbm, resid, loc.at[1]),
        pltpu.make_async_copy(proj_hbm, proj, loc.at[2]),
        pltpu.make_async_copy(key_hbm, kx_hbm.at[pl.ds(span * seq_dev, seq_dev), :], loc.at[3]),
        pltpu.make_async_copy(value_hbm, vx_hbm.at[pl.ds(span * seq_dev, seq_dev), :], loc.at[4]),
    ]
    for c in range(chunks):
        for d in (4, 5, 3, 2, 6, 1, 7):
            a2a(c, d).start()
        if c == 0:
            for copy in local:
                copy.start()

    def kv(d, which):
        src, dst = ((key_hbm, kx_hbm), (value_hbm, vx_hbm))[which]
        return pltpu.make_async_remote_copy(
            src_ref=src,
            dst_ref=dst.at[pl.ds((span - d) * seq_dev, seq_dev), :],
            send_sem=kv_send.at[d - 1, which],
            recv_sem=kv_recv.at[d - 1, which],
            device_id=(seq + d, me),
            device_id_type=MESH,
        )

    for d in range(1, span + 1):
        @pl.when(seq + d < n_seq)
        def _():
            kv(d, 0).start()
            kv(d, 1).start()

    ids = ids_ref[...]
    lane = lax.broadcasted_iota(jnp.int32, (tok, heads * cap), 1)
    expert, rank = lane // cap, lax.rem(lane, cap)
    hits = [(ids[:, k : k + 1] == expert) for k in range(2)]
    both = (hits[0] | hits[1]).astype(jnp.float32).astype(jnp.bfloat16)
    before = (lax.broadcasted_iota(jnp.int32, (tok, tok), 1) < lax.broadcasted_iota(jnp.int32, (tok, tok), 0))
    count = jnp.dot(before.astype(jnp.float32).astype(jnp.bfloat16), both, preferred_element_type=jnp.float32)
    here = count == rank.astype(jnp.float32)
    for k in range(2):
        pick[k] = (hits[k] & here).astype(jnp.float32).astype(jnp.bfloat16)
    for h in range(attn_ref.shape[0]):
        attn_t[h * 128 : (h + 1) * 128, :] = attn_ref[h].T
    acc[...] = jnp.zeros_like(acc)
    gates = gates_ref[...]
    for copy in local:
        copy.wait()

    def send(c, p, o, dz, flip, slot):
        block = hid.at[pl.ds(pl.multiple_of(o * tok, tok), tok), pl.ds(c * w + p * piece, piece)]
        return pltpu.make_async_remote_copy(
            src_ref=block,
            dst_ref=block,
            send_sem=ag_send.at[c, p, slot],
            recv_sem=ag_recv.at[c, p, o],
            device_id=(seq, at(dz, flip)),
            device_id_type=MESH,
        )

    def arrived(c, p, o):
        block = hid.at[pl.ds(pl.multiple_of(o * tok, tok), tok), pl.ds(c * w + p * piece, piece)]
        pltpu.make_async_remote_copy(
            src_ref=block, dst_ref=block, send_sem=ag_send.at[c, p, 0], recv_sem=ag_recv.at[c, p, o],
            device_id=(seq, at(0, True)), device_id_type=MESH,
        ).wait_recv()

    def first(c):
        for p in range(4):
            send(c, p, me, 0, True, 0).start()
            send(c, p, me, 1, False, 1).start()
            send(c, p, me, 3, False, 2).start()

    def second(c):
        for p in range(4):
            back, on = (3, 1) if p % 2 == 0 else (1, 3)
            arrived(c, p, at(back, False))
            send(c, p, at(back, False), on, False, 3).start()
            if p < 2:
                arrived(c, p, at(0, True))
                send(c, p, at(0, True), 1, False, 4).start()
                send(c, p, at(0, True), 3, False, 5).start()
            else:
                send(c, p, at(back, False), 0, True, 4).start()
                arrived(c, p, at(on, False))
                send(c, p, at(on, False), 0, True, 5).start()

    def third(c):
        for p in range(4):
            back, on = (3, 1) if p % 2 == 0 else (1, 3)
            if p < 2:
                arrived(c, p, at(back, True))
                send(c, p, at(back, True), on, False, 6).start()
            else:
                arrived(c, p, at(2, False))
                send(c, p, at(2, False), 0, True, 6).start()

    def rest(c):
        for p in range(4):
            back, on = (3, 1) if p % 2 == 0 else (1, 3)
            if p < 2:
                arrived(c, p, at(on, False))
                arrived(c, p, at(2, False))
                arrived(c, p, at(on, True))
                arrived(c, p, at(2, True))
            else:
                arrived(c, p, at(0, True))
                for dz in (1, 2, 3):
                    arrived(c, p, at(dz, True))

    def combine(c):
        for d in range(1, heads):
            a2a(c, d).wait_recv()
        tile = 256

        def body(t, _):
            cols = pl.ds(pl.multiple_of(c * w + t * tile, tile), tile)
            got = recv[:, cols]
            total = resid[:, cols].astype(jnp.float32)
            for k in range(2):
                total = total + gates[:, k : k + 1] * jnp.dot(pick[k], got, preferred_element_type=jnp.float32)
            hid[pl.ds(pl.multiple_of(me * tok, tok), tok), cols] = total.astype(jnp.bfloat16)
            return 0

        lax.fori_loop(0, w // tile, body, 0)

    def multiply(c):
        def rows_body(r, _):
            rows = pl.ds(pl.multiple_of(r * 256, 256), 256)
            acc[rows, :] += lax.dot_general(
                hid[rows, c * w : (c + 1) * w], proj[:, c * w : (c + 1) * w], NEAR,
                preferred_element_type=jnp.float32,
            )
            return 0

        lax.fori_loop(0, heads * tok // 256, rows_body, 0)

        def cols_body(t, _):
            cols = pl.ds(pl.multiple_of(c * w + t * 256, 256), 256)
            gproj_ref[:, cols] = jnp.dot(attn_t[...], hid[:, cols], preferred_element_type=jnp.float32).astype(jnp.bfloat16)
            return 0

        lax.fori_loop(0, w // 256, cols_body, 0)

    for t in range(chunks + 3):
        if t < chunks:
            combine(t)
            first(t)
        if 0 <= t - 1 < chunks:
            second(t - 1)
        if 0 <= t - 2 < chunks:
            third(t - 2)
        if 0 <= t - 3 < chunks:
            rest(t - 3)
            multiply(t - 3)
    gout_ref[...] = acc[...].astype(jnp.bfloat16)

    for c in range(chunks):
        for d in range(1, heads):
            a2a(c, d).wait_send()
        for p in range(4):
            for slot in range(7):
                send(c, p, me, 0, True, slot).wait_send()
    for d in range(1, span + 1):
        @pl.when(seq + d < n_seq)
        def _():
            kv(d, 0).wait_send()
            kv(d, 1).wait_send()
        @pl.when(seq >= d)
        def _():
            kv(d, 0).wait_recv()
            kv(d, 1).wait_recv()


def gathered(rows, ids, gates, resid, proj, attn, keys, values, chunks=4):
    tok, width = resid.shape
    heads = lax.axis_size("head")
    n, seq_dev, dim = attn.shape
    span = (WIN + seq_dev - 1) // seq_dev
    bf = jnp.bfloat16
    anyspace = pl.BlockSpec(memory_space=pl.ANY)
    vmem = pl.BlockSpec(memory_space=pltpu.VMEM)
    return pl.pallas_call(
        functools.partial(gather_kernel, chunks),
        out_shape=[
            jax.ShapeDtypeStruct((seq_dev, n * dim), bf),
            jax.ShapeDtypeStruct((n * dim, width), bf),
            jax.ShapeDtypeStruct(((span + 1) * seq_dev, dim), bf),
            jax.ShapeDtypeStruct(((span + 1) * seq_dev, dim), bf),
        ],
        in_specs=[anyspace, vmem, vmem, anyspace, anyspace, vmem, anyspace, anyspace],
        out_specs=[vmem, vmem, anyspace, anyspace],
        scratch_shapes=[
            pltpu.VMEM(rows.shape, bf),
            pltpu.VMEM((heads * tok, width), bf),
            pltpu.VMEM(proj.shape, bf),
            pltpu.VMEM((n * dim, seq_dev), bf),
            pltpu.VMEM((tok, width), bf),
            pltpu.VMEM((2, tok, rows.shape[0]), bf),
            pltpu.VMEM((seq_dev, n * dim), jnp.float32),
            pltpu.SemaphoreType.DMA((chunks, heads - 1)),
            pltpu.SemaphoreType.DMA((chunks, heads - 1)),
            pltpu.SemaphoreType.DMA((chunks, 4, 7)),
            pltpu.SemaphoreType.DMA((chunks, 4, heads)),
            pltpu.SemaphoreType.DMA((span, 2)),
            pltpu.SemaphoreType.DMA((span, 2)),
            pltpu.SemaphoreType.DMA((5,)),
        ],
        compiler_params=pltpu.CompilerParams(
            collective_id=0, has_side_effects=True, vmem_limit_bytes=56 * 2**20
        ),
        cost_estimate=pl.CostEstimate(flops=10**10, bytes_accessed=50 * 2**20, transcendentals=0),
        name="combine_gather_project",
    )(rows, ids, gates, resid, proj, attn, keys, values)


def window_kernel(block, first_ref, q_ref, do_ref, k_ref, v_ref, kt_ref, lse_ref, delta_ref, dq_ref, dk_ref, dv_ref, dq_acc):
    groups = q_ref.shape[0]
    i = pl.program_id(0)
    scale = 1.0 / math.sqrt(128)

    @pl.when(i == 0)
    def _():
        dk_ref[...] = jnp.zeros_like(dk_ref)
        dv_ref[...] = jnp.zeros_like(dv_ref)

    dq_acc[...] = jnp.zeros_like(dq_acc)
    last = i + WIN // block

    def step(kb, mask):
        rows = pl.ds(pl.multiple_of(kb * block, block), block)
        k = k_ref[rows, :]
        v = v_ref[rows, :]
        dv = jnp.zeros((block, 128), jnp.float32)
        dk = jnp.zeros((block, 128), jnp.float32)
        for h in range(groups):
            q = q_ref[h]
            do = do_ref[:, h * 128 : (h + 1) * 128]
            s = lax.dot_general(k, q, NEAR, preferred_element_type=jnp.float32)
            dp = lax.dot_general(v, do, NEAR, preferred_element_type=jnp.float32)
            p = jnp.exp2(s * (LOG2E * scale) - lse_ref[h : h + 1, :])
            if mask is not None:
                p = jnp.where(mask, p, 0.0)
            ds = p * (dp - delta_ref[h : h + 1, :])
            pb = p.astype(jnp.bfloat16)
            db = ds.astype(jnp.bfloat16)
            dv = dv + jnp.dot(pb, do, preferred_element_type=jnp.float32)
            dk = dk + jnp.dot(db, q, preferred_element_type=jnp.float32)
            dq_acc[h] += jnp.dot(kt_ref[:, rows], db, preferred_element_type=jnp.float32)
        dv_ref[rows, :] += dv
        dk_ref[rows, :] += dk * scale

    key = lax.broadcasted_iota(jnp.int32, (block, block), 0)
    query = lax.broadcasted_iota(jnp.int32, (block, block), 1)
    start = first_ref[0]

    @pl.when(start <= i)
    def _():
        step(i, key > query)

    def loop(kb, _):
        step(kb, None)
        return 0

    lax.fori_loop(jnp.maximum(i + 1, start), last, loop, 0)
    step(last, key <= query)
    for h in range(groups):
        dq_ref[:, h * 128 : (h + 1) * 128] = (dq_acc[h].T * scale).astype(jnp.bfloat16)


def window_backward(first_key, q, do, kx, vx, lse, delta, block=512):
    groups, tokens, dim = q.shape
    keys = kx.shape[0]

    def full(shape):
        return pl.BlockSpec(shape, lambda i, *_: (0,) * len(shape))

    return pl.pallas_call(
        functools.partial(window_kernel, block),
        grid_spec=pltpu.PrefetchScalarGridSpec(
            num_scalar_prefetch=1,
            grid=(tokens // block,),
            in_specs=[
                pl.BlockSpec((groups, block, dim), lambda i, *_: (0, i, 0)),
                pl.BlockSpec((block, groups * dim), lambda i, *_: (i, 0)),
                full(kx.shape),
                full(vx.shape),
                full((dim, keys)),
                pl.BlockSpec((groups, block), lambda i, *_: (0, i)),
                pl.BlockSpec((groups, block), lambda i, *_: (0, i)),
            ],
            out_specs=[
                pl.BlockSpec((block, groups * dim), lambda i, *_: (i, 0)),
                full((keys, dim)),
                full((keys, dim)),
            ],
            scratch_shapes=[pltpu.VMEM((groups, dim, block), jnp.float32)],
        ),
        out_shape=[
            jax.ShapeDtypeStruct((tokens, groups * dim), jnp.bfloat16),
            jax.ShapeDtypeStruct((keys, dim), jnp.float32),
            jax.ShapeDtypeStruct((keys, dim), jnp.float32),
        ],
        compiler_params=pltpu.CompilerParams(vmem_limit_bytes=40 * 2**20),
        cost_estimate=pl.CostEstimate(
            flops=10 * groups * tokens * WIN * dim, bytes_accessed=10 * 2**20,
            transcendentals=groups * tokens * WIN,
        ),
        name="window_backward",
    )((first_key // block).reshape(1), q, do, kx, vx, kx.T, lse * LOG2E, delta)


def shifted(block, axis, distance):
    devices = range(lax.axis_size(axis))
    route = [(i - distance, i) for i in devices if i - distance in devices]
    return lax.ppermute(block, axis, route)


def local(
    out_grad, expert_rows, expert_ids, gates, out_proj, attention_output,
    saved_queries, saved_keys, saved_values, softmax_normalizer,
):
    heads_dev, seq_dev, head_dim = saved_queries.shape
    span = (WIN + seq_dev - 1) // seq_dev
    heads = lax.axis_size("head")
    grad_out, proj_part, kx, vx = gathered(
        expert_rows[0], expert_ids, gates, out_grad, out_proj, attention_output, saved_keys[0], saved_values[0]
    )
    part = lax.psum_scatter(proj_part, "seq", scatter_dimension=0, tiled=True)
    grad_proj = lax.all_gather(part, "seq", axis=0, tiled=True)
    head_grads = jnp.transpose(grad_out.reshape(seq_dev, heads_dev, head_dim), (1, 0, 2))
    delta = jnp.sum(head_grads.astype(jnp.float32) * attention_output.astype(jnp.float32), axis=2)
    seq_pos = lax.axis_index("seq").astype(jnp.int32)
    first_key = jnp.maximum(span - seq_pos, 0) * seq_dev
    dq, dk_ext, dv_ext = window_backward(first_key, saved_queries, grad_out, kx, vx, softmax_normalizer, delta)
    ext = jnp.concatenate([dk_ext, dv_ext], axis=1)
    total = ext[span * seq_dev :]
    for distance in range(1, span + 1):
        far = ext[(span - distance) * seq_dev : (span - distance + 1) * seq_dev].astype(jnp.bfloat16)
        total = total + shifted(far, "seq", -distance).astype(jnp.float32)
    mine = jnp.concatenate([dq, total.astype(jnp.bfloat16)], axis=1)
    tok = seq_dev // heads
    swapped = lax.all_to_all(mine.reshape(heads, tok, mine.shape[1]), "head", split_axis=0, concat_axis=0, tiled=True)
    rows = jnp.transpose(swapped, (1, 0, 2))
    width = heads_dev * head_dim
    return (
        rows[:, :, :width].reshape(tok, heads * width),
        rows[:, :, width : width + head_dim].reshape(tok, heads * head_dim),
        rows[:, :, width + head_dim :].reshape(tok, heads * head_dim),
        grad_proj,
    )


def solution(mesh):
    in_specs = (
        P(("seq", "head"), None),
        P("head", "seq", None),
        P(("seq", "head"), None),
        P(("seq", "head"), None),
        P("head", None),
        P("head", "seq", None),
        P("head", "seq", None),
        P("head", "seq", None),
        P("head", "seq", None),
        P("head", "seq"),
    )
    out_specs = (
        P(("seq", "head"), None),
        P(("seq", "head"), None),
        P(("seq", "head"), None),
        P("head", None),
    )
    return jax.shard_map(local, mesh=mesh, in_specs=in_specs, out_specs=out_specs, check_vma=False)
```

time: 768 us -> 438 us (0.57); the launches traced: 757 us -> 438 us
  Pallas kernels: 0 us -> 261 us
  waiting for transfers between devices: 309 us -> 115 us
  matrix products: 115 us -> 0 us
  blocking collectives: 126 us -> 21.5 us
  local copies, waits for them, and re-layouts: 97.2 us -> 16.2 us
  other arithmetic: 51.5 us -> 2.57 us
  starting transfers between devices: 42.4 us -> 7.94 us
    pallas_call x0 -> x2, Pallas kernels: none -> 261 us  [the longest x1 222 us: gathered(): pl.pallas_call(functools.partial(gather_kernel, chunks), out_shape=[jax.S...]
    psum x1 -> x0, blocking collectives: 126 us -> none  [local(): summed_proj = lax.psum(partial_value, 'seq')]
    dot_general x32 -> x0, matrix products: 115 us -> none  [the longest x6 25.6 us: block_step(): lax.dot_general(query_blk, key_blk, (((1,), (1,)), ((), ())), preferred_e...]
    all_gather x1, waiting for transfers between devices: 109 us -> 0.01 us  [local(): grad_proj = lax.all_gather(part, 'seq', axis=0, tiled=True)]
    ppermute x8 -> x4, waiting for transfers between devices: 130 us -> 43.4 us  [shifted(): return lax.ppermute(block, axis, route)]
    reduce_scatter x0 -> x1, waiting for transfers between devices: none -> 71.1 us  [local(): part = lax.psum_scatter(proj_part, 'seq', scatter_dimension=0, tiled=True)]
    all_to_all x4 -> x0, waiting for transfers between devices: 69.8 us -> none  [the longest x1 69.8 us: local(): lax.all_to_all(expert_rows, 'head', split_axis=1, concat_axis=0, tiled=True)]
    unnamed x31 -> x19, local copies, waits for them, and re-layouts: 55.6 us -> 11.9 us
  transfers between devices with their start and end apart: 13 -> 6, of which waited for: 8 -> 5; matrix products, arithmetic and copies ran while one was open for 4% -> 2% of each run, Pallas kernels for 0% -> 9%
where the time goes in v1:
time: 438 us
  Pallas kernels  261 us (60%)
  waiting for transfers between devices  115 us (26%)
  blocking collectives  21.5 us (5%)
  local copies, waits for them, and re-layouts  16.2 us (4%)
  between operations  14.2 us (3%)
  starting transfers between devices  7.94 us (2%)
    pallas_call x1, Pallas kernels, gathered(): pl.pallas_call(functools.partial(gather_kernel, chunks), out_shape=[jax.S...  222 us
    reduce_scatter x1, waiting for transfers between devices, local(): part = lax.psum_scatter(proj_part, 'seq', scatter_dimension=0, tiled=True)  71.1 us
    ppermute x4, waiting for transfers between devices, shifted(): return lax.ppermute(block, axis, route)  43.4 us
    pallas_call x1, Pallas kernels, window_backward(): pl.pallas_call(functools.partial(window_kernel, block), grid_spec=pltpu.P...  38.7 us
    all_to_all x1, blocking collectives, local(): lax.all_to_all(mine.reshape(heads, tok, mine.shape[1]), 'head', split_axi...  21.5 us
    unnamed x19, local copies, waits for them, and re-layouts  11.9 us
  transfers between devices with their start and end apart: 6, of which 5 were waited for; matrix products, arithmetic and copies ran while one was open for 2% of the time, Pallas kernels for 9%

profile of v1, /device:TPU:24, one launch (start us, length us, event | category | flops | bytes accessed | tf_op | source)
XLA Modules:
  0.0 437.9 jit_solution(11304524690201467493)
XLA Ops:
  7.2 1.4 copy.21.ids_ref
  8.6 1.4 copy.22.gates_ref
  10.0 222.2 %combine_gather_project.1 = (bf16[1024,384]{1,0:T(8,128)(2,1)}, bf16[384,6144]{1,0:T(8,128)(2,1)}, bf16[5120,128]{1,0:T(8,128)(2,1)}, bf16[5120,128]{1,0:T(8,128)(2,1)}) custom-call(bf16[512,6144]{1,0:T(8,128)(2,1)} %bitcast.27, s32[128,2]{1,0:T(8,128)} %copy.21.ids_ref, f32[128,2]{1,0:T(8,128)} %copy.22.gates_ref, bf16[128,6144]{1,0:T(8,128)(2,1)} %resid_hbm.1, ...), custom_call_target="tpu_custom_call" | custom-call | flops 10000000000 | bytes 52428800 | tf_op jit(solution)/shard_map/combine_gather_project/pallas_call | solution.py:242
  232.3 0.2 all-gather.2.cloned.1.call-start
  232.5 71.1 %reduce-scatter.2.cloned.1.call-done = bf16[24,6144]{1,0:T(8,128)(2,1)} async-done(((bf16[384,6144]{1,0:T(8,128)(2,1)}), bf16[24,6144]{1,0:T(8,128)(2,1)}) %reduce-scatter.2.cloned.1.call-update) | async-done | bytes 294928 | tf_op jit(solution)/shard_map/reduce_scatter | solution.py:388
  303.7 1.2 copy.25
  304.9 0.6 copy.23
  305.5 1.4 copy.24
  306.9 1.8 multiply_reduce_fusion.delta_ref
  308.8 1.1 copy-done.2
  309.9 1.3 copy-done.3
  311.2 38.7 %window_backward.1 = (bf16[1024,384]{1,0:T(8,128)(2,1)S(1)}, f32[5120,128]{1,0:T(8,128)S(1)}, f32[5120,128]{1,0:T(8,128)S(1)}) custom-call(s32[1]{0:T(128)} %bitcast.first_ref, bf16[3,1024,128]{2,1,0:T(8,128)(2,1)S(1)} %copy-done.2, bf16[1024,384]{1,0:T(8,128)(2,1)S(1)} %copy-done.1, bf16[5120,128]{1,0:T(8,128)(2,1)S(1)} %copy-done, ...), custom_call_target="tpu_custom_call" | custom-call | flops 16106127360 | bytes 10485760 | tf_op jit(solution)/shard_map/window_backward/pallas_call | solution.py:337
  350.0 0.2 constant_dynamic-update-slice_fusion.1
  350.2 0.2 constant_dynamic-update-slice_fusion
  350.4 0.3 convert.8
  350.6 0.1 fusion.4
  350.8 1.9 collective-permute-start
  352.7 1.9 collective-permute-start.3
  354.6 1.9 collective-permute-start.2
  356.6 1.9 collective-permute-start.1
  358.5 2.9 collective-permute-done
  361.4 16.3 %collective-permute-done.3 = bf16[1024,256]{1,0:T(8,128)(2,1)S(1)} collective-permute-done((bf16[1024,256]{1,0:T(8,128)(2,1)S(1)}, bf16[1024,256]{1,0:T(8,128)(2,1)S(1)}, u32[]{:S(2)}, u32[]{:S(2)}) %collective-permute-start.3) | collective-permute-done | bytes 524320 | tf_op jit(solution)/shard_map/ppermute | solution.py:375
  377.7 8.3 %collective-permute-done.2 = bf16[1024,256]{1,0:T(8,128)(2,1)S(1)} collective-permute-done((bf16[1024,256]{1,0:T(8,128)(2,1)S(1)}, bf16[1024,256]{1,0:T(8,128)(2,1)S(1)}, u32[]{:S(2)}, u32[]{:S(2)}) %collective-permute-start.2) | collective-permute-done | bytes 524320 | tf_op jit(solution)/shard_map/ppermute | solution.py:375
  386.0 16.0 %collective-permute-done.1 = bf16[1024,256]{1,0:T(8,128)(2,1)S(1)} collective-permute-done((bf16[1024,256]{1,0:T(8,128)(2,1)S(1)}, bf16[1024,256]{1,0:T(8,128)(2,1)S(1)}, u32[]{:S(2)}, u32[]{:S(2)}) %collective-permute-start.1) | collective-permute-done | bytes 524320 | tf_op jit(solution)/shard_map/ppermute | solution.py:375
  401.9 0.3 fusion.3
  402.2 0.1 pad_maximum_fusion
  402.4 21.5 %all_to_all.5 = bf16[8,128,640]{2,1,0:T(8,128)(2,1)S(1)} all-to-all(bf16[8,128,640]{2,1,0:T(8,128)(2,1)S(1)} %bitcast.25), channel_id=1, replica_groups=mesh['seq'=16,'head'=8] {'head'}, dimensions={0} | all-to-all | bytes 2621440 | tf_op jit(solution)/shard_map/all_to_all | solution.py:402
  423.9 0.1 slice_bitcast_fusion
  424.0 1.0 copy.29
  425.0 0.1 slice_bitcast_fusion.1
  425.2 0.9 copy_bitcast_fusion
  426.0 5.1 %copy.36 = bf16[384,6144]{1,0:T(8,128)(2,1)} copy(bf16[384,6144]{1,0:T(8,128)(2,1)} %all-gather.2.cloned.1.call-done) | data formatting | bytes 9437184
  (15 shorter events, 0.1 us)
Async XLA Ops:
  7.2 296.5 %reduce-scatter.2.cloned.1.call-start = ((), (), s32[]{:S(2)}) async-start(), calls=%async_computation.2 | async-start | bytes 5013504 | tf_op jit(solution)/shard_map/reduce_scatter | solution.py:388
  232.2 71.4 %copy-start.4 = (bf16[3,1024,128]{2,1,0:T(8,128)(2,1)S(1)}, bf16[3,1024,128]{2,1,0:T(8,128)(2,1)}, u32[]{:S(2)}) copy-start(bf16[3,1024,128]{2,1,0:T(8,128)(2,1)} %attn_ref.1) | copy-start | bytes 2359300
  232.2 72.6 %copy-start = (bf16[5120,128]{1,0:T(8,128)(2,1)S(1)}, bf16[5120,128]{1,0:T(8,128)(2,1)}, u32[]{:S(2)}) copy-start(bf16[5120,128]{1,0:T(8,128)(2,1)} %get-tuple-element.12.k_ref) | copy-start | bytes 3932164
  232.3 73.2 %copy-start.1 = (bf16[1024,384]{1,0:T(8,128)(2,1)S(1)}, bf16[1024,384]{1,0:T(8,128)(2,1)}, u32[]{:S(2)}) copy-start(bf16[1024,384]{1,0:T(8,128)(2,1)} %get-tuple-element.11.do_ref) | copy-start | bytes 2359300
  232.3 193.8 %all-gather.2.cloned.1.call-start = ((), (), s32[]{:S(2)}) async-start(), calls=%async_computation.3 | async-start | bytes 5013504 | tf_op jit(solution)/shard_map/all_gather | solution.py:389
  305.5 3.3 copy-start.5
  308.8 1.1 copy-start.2
  309.9 1.3 copy-start.3
  350.8 10.6 %collective-permute-start = (bf16[1024,256]{1,0:T(8,128)(2,1)S(1)}, bf16[1024,256]{1,0:T(8,128)(2,1)S(1)}, u32[]{:S(2)}, u32[]{:S(2)}) collective-permute-start(bf16[1024,256]{1,0:T(8,128)(2,1)S(1)} %get-tuple-element.18), channel_id=1, source_target_pairs={{8,0},{16,8},{24,16},{32,24},{40,32},{48,40},{56,48},{64,56},{72,6... | collective-permute-start | bytes 1572872 | tf_op jit(solution)/shard_map/ppermute | solution.py:375
  352.7 25.0 %collective-permute-start.3 = (bf16[1024,256]{1,0:T(8,128)(2,1)S(1)}, bf16[1024,256]{1,0:T(8,128)(2,1)S(1)}, u32[]{:S(2)}, u32[]{:S(2)}) collective-permute-start(bf16[1024,256]{1,0:T(8,128)(2,1)S(1)} %get-tuple-element.19), channel_id=1, source_target_pairs={{32,0},{40,8},{48,16},{56,24},{64,32},{72,40},{80,48},{88,56},{96,... | collective-permute-start | bytes 1572872 | tf_op jit(solution)/shard_map/ppermute | solution.py:375
  354.6 31.3 %collective-permute-start.2 = (bf16[1024,256]{1,0:T(8,128)(2,1)S(1)}, bf16[1024,256]{1,0:T(8,128)(2,1)S(1)}, u32[]{:S(2)}, u32[]{:S(2)}) collective-permute-start(bf16[1024,256]{1,0:T(8,128)(2,1)S(1)} %get-tuple-element.20), channel_id=1, source_target_pairs={{24,0},{32,8},{40,16},{48,24},{56,32},{64,40},{72,48},{80,56},{88,... | collective-permute-start | bytes 1572872 | tf_op jit(solution)/shard_map/ppermute | solution.py:375
  356.6 45.3 %collective-permute-start.1 = (bf16[1024,256]{1,0:T(8,128)(2,1)S(1)}, bf16[1024,256]{1,0:T(8,128)(2,1)S(1)}, u32[]{:S(2)}, u32[]{:S(2)}) collective-permute-start(bf16[1024,256]{1,0:T(8,128)(2,1)S(1)} %get-tuple-element.21), channel_id=1, source_target_pairs={{16,0},{24,8},{32,16},{40,24},{48,32},{56,40},{64,48},{72,56},{80,... | collective-permute-start | bytes 1572872 | tf_op jit(solution)/shard_map/ppermute | solution.py:375
Sparse Core Ops, SparseCore 0:
  232.4 71.1 reduce-scatter.1
  305.3 40.2 all-gather.1

commit v2 on v0

v2 whole, which is shorter than its diff:
```python
import functools
import math

import jax
import jax.numpy as jnp
from jax import lax
from jax.experimental import pallas as pl
from jax.experimental.pallas import tpu as pltpu
from jax.sharding import PartitionSpec as P

WIN = 4096
LOG2E = 1.4426950408889634
MESH = pl.DeviceIdType.MESH
NEAR = (((1,), (1,)), ((), ()))
BF = jnp.bfloat16
F32 = jnp.float32

NZ, NY = 4, 4
HEADS = 8
CHUNKS = 4
HALVES = 2
SPAN = 4
BLK = 512
UNITS = ((0, 0), (1, 0), (0, 1), (1, 1), (0, 2), (0, 3), (1, 2), (1, 3))


def layer_kernel(
    rows_hbm, ids_ref, gates_ref, resid_hbm, proj_hbm, attn_hbm, q_hbm, key_hbm, value_hbm, lse_ref,
    dq_hbm, dk_hbm, dv_hbm, gproj_hbm,
    recv, hid, proj, attn, attn_t, resid, pick, acc, gout, delta, qv, kx, vx, kt, dk, dv, dq_acc, dqs,
    r1, r2, s2, t3, r3, gfin, kvs, rc, rm1, rm2, kvf,
    a2a_send, a2a_recv, ag_send, ag_recv, kv_send, kv_recv,
    gp_send, gp_recv, dq_send, dq_recv, dkv_send, dkv_recv, fin_send, fin_recv, loc, loc_q, loc_out,
):
    seq = lax.axis_index("seq")
    me = lax.axis_index("head")
    n_seq = lax.axis_size("seq")
    z, x = me // 2, lax.rem(me, 2)
    core = lax.rem(seq, 2)
    y = lax.rem(seq // 2, NY)
    xlo = seq // (2 * NY)
    tok, width = resid.shape
    sub = tok // HALVES
    half = HEADS * sub
    cap = recv.shape[0] // HEADS
    w = width // CHUNKS
    cuts = (0, w // 3, 2 * w // 3, 5 * w // 6, w)
    wh = w // 2
    n_heads = attn.shape[1]
    dim = 128
    feats = n_heads * dim
    seq_dev = key_hbm.shape[0]
    scale = 1.0 / math.sqrt(dim)

    def mult(v, n):
        return pl.multiple_of(v, n)

    def at(dz, flip):
        return lax.rem(z + dz, NZ) * 2 + (lax.rem(x + 1, 2) if flip else x)

    sibling = seq + 1 - 2 * core
    across = lax.rem(seq + 2 * NY, 4 * NY)

    def along_y(d):
        return xlo * 2 * NY + lax.rem(y + d, NY) * 2 + core

    barrier = pltpu.get_barrier_semaphore()

    def greet(s, h):
        pl.semaphore_signal(barrier, inc=1, device_id=(s, h), device_id_type=MESH)

    for d in range(1, HEADS):
        greet(seq, lax.rem(me + d, HEADS))
    for d in range(1, 8):
        greet(lax.rem(seq + 2 * d, n_seq), me)
    greet(sibling, me)
    pl.semaphore_wait(barrier, HEADS - 1 + 8)

    def remote(src, dst, send, recv_sem, s, h):
        return pltpu.make_async_remote_copy(
            src_ref=src, dst_ref=dst, send_sem=send, recv_sem=recv_sem, device_id=(s, h), device_id_type=MESH
        )

    def a2a(c, d):
        peer = lax.rem(me + d, HEADS)
        return remote(
            rows_hbm.at[pl.ds(mult(peer * cap, cap), cap), pl.ds(c * w, w)],
            recv.at[pl.ds(mult(me * cap, cap), cap), pl.ds(c * w, w)],
            a2a_send.at[c, d - 1], a2a_recv.at[c, d - 1], seq, peer,
        )

    own = pl.ds(mult(me * cap, cap), cap)
    last_rows = pl.ds(SPAN * seq_dev, seq_dev)
    local = [
        pltpu.make_async_copy(rows_hbm.at[own, :], recv.at[own, :], loc.at[0]),
        pltpu.make_async_copy(resid_hbm, resid, loc.at[1]),
        pltpu.make_async_copy(proj_hbm, proj, loc.at[2]),
        pltpu.make_async_copy(key_hbm, kx.at[last_rows, :], loc.at[3]),
        pltpu.make_async_copy(value_hbm, vx.at[last_rows, :], loc.at[4]),
    ]
    for g in range(HALVES):
        for o in range(HEADS):
            there = pl.ds(o * tok + g * sub, sub)
            here = pl.ds(o * sub, sub)
            local.append(pltpu.make_async_copy(q_hbm.at[:, there, :], qv.at[g, :, here, :], loc_q.at[0, g, o]))
            local.append(pltpu.make_async_copy(attn_hbm.at[:, there, :], attn.at[g, :, here, :], loc_q.at[1, g, o]))
    def kv(k, which):
        arg, ext = ((key_hbm, kx), (value_hbm, vx))[which]
        sems = (kv_send.at[k, which], kv_recv.at[k, which])

        def slot(d):
            return ext.at[pl.ds(mult((SPAN - d) * seq_dev, seq_dev), seq_dev), :]

        if k == 0:
            return remote(arg, slot(2), *sems, seq + 2, me)
        if k == 1:
            return remote(arg, slot(4), *sems, seq + 4, me)
        if k == 2:
            return remote(slot(2 * core), slot(1), *sems, sibling, me)
        return remote(slot(2 + 2 * core), slot(3), *sems, sibling, me)

    def kv_start():
        @pl.when(seq + 4 < n_seq)
        def _():
            kv(1, 0).start()
            kv(1, 1).start()

        @pl.when(seq + 2 < n_seq)
        def _():
            kv(0, 0).start()
            kv(0, 1).start()

    def kv_pass():
        @pl.when(seq >= 2)
        def _():
            kv(0, 0).wait_recv()
            kv(0, 1).wait_recv()

        @pl.when(seq >= 4)
        def _():
            kv(1, 0).wait_recv()
            kv(1, 1).wait_recv()

        @pl.when((core == 0) | (seq >= 2))
        def _():
            kv(2, 0).start()
            kv(2, 1).start()

        @pl.when(seq >= 2 + 2 * core)
        def _():
            kv(3, 0).start()
            kv(3, 1).start()

    for c in range(CHUNKS):
        for d in (4, 5, 3, 2, 6, 1, 7):
            a2a(c, d).start()
        if c == 0:
            kv_start()
            for copy in local:
                copy.start()

    lane = lax.broadcasted_iota(jnp.int32, (tok, HEADS * cap), 1)
    expert, rank = (lane // cap).astype(F32), lax.rem(lane, cap).astype(F32)
    repeats = HEADS * cap // tok
    gates, hits = [], []
    for k in range(2):
        gates.append(jnp.broadcast_to(gates_ref[k : k + 1, :], (tok, tok)).T[:, 0:1])
        named = jnp.broadcast_to(ids_ref[k : k + 1, :].astype(F32), (tok, tok)).T
        hits.append(jnp.concatenate([named] * repeats, axis=1) == expert)
    both = (hits[0] | hits[1]).astype(F32).astype(BF)
    before = lax.broadcasted_iota(jnp.int32, (tok, tok), 1) < lax.broadcasted_iota(jnp.int32, (tok, tok), 0)
    count = jnp.dot(before.astype(F32).astype(BF), both, preferred_element_type=F32)
    here = count == rank
    for k in range(2):
        pick[k] = (hits[k] & here).astype(F32).astype(BF)
    acc[...] = jnp.zeros_like(acc)
    dk[...] = jnp.zeros_like(dk)
    dv[...] = jnp.zeros_like(dv)
    dq_acc[...] = jnp.zeros_like(dq_acc)
    for copy in local:
        copy.wait()
    for g in range(HALVES):
        for h in range(n_heads):
            attn_t[h * dim : (h + 1) * dim, g * half : (g + 1) * half] = attn[g, h].T

    def block(u, p, o):
        g, c = UNITS[u]
        return hid.at[pl.ds(mult(g * half + o * sub, sub), sub), pl.ds(c * w + cuts[p], cuts[p + 1] - cuts[p])]

    def send(u, p, o, dz, flip):
        return remote(block(u, p, o), block(u, p, o), ag_send.at[u], ag_recv.at[u, p, o], seq, at(dz, flip))

    def arrived(u, p, o):
        send(u, p, o, 0, True).wait_recv()

    def ways(p):
        return (3, 1) if p % 2 == 0 else (1, 3)

    def first(u):
        for p in range(4):
            send(u, p, me, 0, True).start()
            send(u, p, me, 1, False).start()
            send(u, p, me, 3, False).start()

    def second(u):
        for p in range(4):
            back, on = ways(p)
            arrived(u, p, at(back, False))
            send(u, p, at(back, False), on, False).start()
            if p < 2:
                arrived(u, p, at(0, True))
                send(u, p, at(0, True), 1, False).start()
                send(u, p, at(0, True), 3, False).start()
            else:
                send(u, p, at(back, False), 0, True).start()
                arrived(u, p, at(on, False))
                send(u, p, at(on, False), 0, True).start()

    def third(u):
        for p in range(4):
            back, on = ways(p)
            if p < 2:
                arrived(u, p, at(back, True))
                send(u, p, at(back, True), on, False).start()
            else:
                arrived(u, p, at(2, False))
                send(u, p, at(2, False), 0, True).start()

    def rest(u):
        for p in range(4):
            back, on = ways(p)
            if p < 2:
                arrived(u, p, at(on, False))
                arrived(u, p, at(2, False))
                arrived(u, p, at(on, True))
                arrived(u, p, at(2, True))
            else:
                for dz in range(NZ):
                    arrived(u, p, at(dz, True))

    def combine(c):
        for d in range(1, HEADS):
            a2a(c, d).wait_recv()
        tile = 256

        def body(t, _):
            cols = pl.ds(mult(c * w + t * tile, tile), tile)
            got = recv[:, cols]
            total = resid[:, cols].astype(F32)
            for k in range(2):
                total = total + gates[k] * jnp.dot(pick[k], got, preferred_element_type=F32)
            total = total.astype(BF)
            for g in range(HALVES):
                hid[pl.ds(mult(g * half + me * sub, sub), sub), cols] = total[g * sub : (g + 1) * sub]
            return 0

        lax.fori_loop(0, w // tile, body, 0)

    def project(u):
        g, c = UNITS[u]

        def body(r, _):
            rows = pl.ds(mult(r * 256, 256), 256)
            from_hid = pl.ds(mult(g * half + r * 256, 256), 256)
            acc[g, rows, :] += lax.dot_general(
                hid[from_hid, c * w : (c + 1) * w], proj[:, c * w : (c + 1) * w], NEAR, preferred_element_type=F32
            )
            return 0

        lax.fori_loop(0, half // 256, body, 0)

    def project_end(g):
        gout[g] = acc[g].astype(BF)
        for h in range(n_heads):
            turned = gout[g, :, h * dim : (h + 1) * dim].T.astype(F32)
            kept = attn_t[h * dim : (h + 1) * dim, g * half : (g + 1) * half].astype(F32)
            delta[g, h : h + 1, :] = jnp.sum(turned * kept, axis=0, keepdims=True)

    gpart = recv
    ry = feats // NY
    rx = ry // 2
    row_y = pl.ds(mult(y * ry, 16), ry)

    def mine(c, other=False):
        side = (1 - core) if other else core
        return pl.ds(mult(c * w + side * wh, 128), wh)

    def gp_copy(c, k):
        sems = (gp_send.at[c, k], gp_recv.at[c, k])
        if k == 0:
            return remote(gpart.at[pl.ds(0, feats), mine(c, True)], r1.at[c], *sems, sibling, me)
        if k <= 3:
            peer = pl.ds(mult(lax.rem(y + k, NY) * ry, 16), ry)
            return remote(gpart.at[peer, mine(c)], r2.at[c, k - 1], *sems, along_y(k), me)
        if k == 4:
            return remote(t3.at[c], r3.at[c], *sems, across, me)
        if k == 5:
            spot = gfin.at[pl.ds(mult(y * ry + xlo * rx, 16), rx), mine(c)]
            return remote(spot, spot, *sems, across, me)
        if k <= 8:
            return remote(gfin.at[row_y, mine(c)], gfin.at[row_y, mine(c)], *sems, along_y(k - 5), me)
        return remote(gfin.at[:, mine(c)], gfin.at[:, mine(c)], *sems, sibling, me)

    def gp0(c):
        def body(t, _):
            cols = pl.ds(mult(c * w + t * 256, 256), 256)
            gpart[pl.ds(0, feats), cols] = jnp.dot(attn_t[...], hid[:, cols], preferred_element_type=F32).astype(BF)
            return 0

        lax.fori_loop(0, w // 256, body, 0)
        gp_copy(c, 0).start()

    def gp1(c):
        gp_copy(c, 0).wait_recv()

        def body(r, _):
            rows = pl.ds(mult(r * 48, 16), 48)
            gpart[rows, mine(c)] = (gpart[rows, mine(c)].astype(F32) + r1[c, rows, :].astype(F32)).astype(BF)
            return 0

        lax.fori_loop(0, feats // 48, body, 0)
        for k in (1, 2, 3):
            gp_copy(c, k).start()

    def gp2(c):
        for k in (1, 2, 3):
            gp_copy(c, k).wait_recv()
        total = gpart[row_y, mine(c)].astype(F32)
        for k in range(3):
            total = total + r2[c, k].astype(F32)
        s2[c] = total
        t3[c] = s2[c, pl.ds(mult((1 - xlo) * rx, 16), rx), :].astype(BF)
        gp_copy(c, 4).start()

    def gp3(c):
        gp_copy(c, 4).wait_recv()
        total = s2[c, pl.ds(mult(xlo * rx, 16), rx), :] + r3[c].astype(F32)
        gfin[pl.ds(mult(y * ry + xlo * rx, 16), rx), mine(c)] = total.astype(BF)
        gp_copy(c, 5).start()

    def gp4(c):
        gp_copy(c, 5).wait_recv()
        for k in (6, 7, 8):
            gp_copy(c, k).start()

    def gp5(c):
        for k in (6, 7, 8):
            gp_copy(c, k).wait_recv()
        gp_copy(c, 9).start()

    def gp_out(c):
        return pltpu.make_async_copy(gfin.at[:, pl.ds(c * w, w)], gproj_hbm.at[:, pl.ds(c * w, w)], loc_out.at[c])

    def gp6(c):
        gp_copy(c, 9).wait_recv()
        gp_out(c).start()

    def attend(g, kb, lo, n, masked):
        rows = pl.ds(mult(kb * BLK, BLK), BLK)
        k = kx[rows, :]
        v = vx[rows, :]
        cols = slice(lo, lo + n)
        if masked:
            col = lax.broadcasted_iota(jnp.int32, (BLK, n), 1) + lo
            query = (col // sub) * tok + g * sub + lax.rem(col, sub)
            ago = query + WIN - (lax.broadcasted_iota(jnp.int32, (BLK, n), 0) + kb * BLK)
            keep = (ago >= 0) & (ago < WIN)
        ndv = jnp.zeros((BLK, dim), F32)
        ndk = jnp.zeros((BLK, dim), F32)
        for h in range(n_heads):
            q = qv[g, h, cols, :]
            do = gout[g, cols, h * dim : (h + 1) * dim]
            s = lax.dot_general(k, q, NEAR, preferred_element_type=F32)
            dp = lax.dot_general(v, do, NEAR, preferred_element_type=F32)
            p = jnp.exp2(s * (LOG2E * scale) - lse_ref[g, h : h + 1, cols])
            if masked:
                p = jnp.where(keep, p, 0.0)
            ds = p * (dp - delta[g, h : h + 1, cols])
            pb = p.astype(BF)
            db = ds.astype(BF)
            ndv = ndv + jnp.dot(pb, do, preferred_element_type=F32)
            ndk = ndk + jnp.dot(db, q, preferred_element_type=F32)
            dq_acc[h, :, cols] += jnp.dot(kt[:, rows], db, preferred_element_type=F32)
        dv[rows, :] += ndv
        dk[rows, :] += ndk * scale

    def dq_copy(g, d):
        o = lax.rem(me + d, HEADS)
        src = dqs.at[g, pl.ds(mult(o * sub, sub), sub), :]
        dst = dq_hbm.at[pl.ds(g * sub, sub), pl.ds(mult(me * feats, 128), feats)]
        if d == 0:
            return pltpu.make_async_copy(src, dst, loc_out.at[CHUNKS + g])
        return remote(src, dst, dq_send.at[g, d - 1], dq_recv.at[g, d - 1], seq, o)

    def dq_end(g):
        for h in range(n_heads):
            dqs[g, :, h * dim : (h + 1) * dim] = (dq_acc[h].T * scale).astype(BF)
        dq_acc[...] = jnp.zeros_like(dq_acc)
        for d in range(HEADS):
            dq_copy(g, d).start()

    def far(d):
        return pl.ds((SPAN - d) * seq_dev, seq_dev)

    def dkv_copy(k):
        sems = (dkv_send.at[k], dkv_recv.at[k])
        if k == 0:
            return remote(kvs.at[2], rc.at[0], *sems, sibling, me)
        if k == 1:
            return remote(kvs.at[0], rc.at[1], *sems, sibling, me)
        if k == 2:
            return remote(kvs.at[3], rm2, *sems, seq - 4, me)
        return remote(kvs.at[1], rm1, *sems, seq - 2, me)

    def pack(d, part=None):
        def body(r, _):
            rows = pl.ds(mult(r * 128, 128), 128)
            ext = pl.ds(mult((SPAN - d) * seq_dev + r * 128, 128), 128)
            for side, acc_ref in enumerate((dk, dv)):
                total = acc_ref[ext, :]
                if part is not None:
                    total = total + rc[part, rows, side * dim : (side + 1) * dim].astype(F32)
                kvs[d - 1, rows, side * dim : (side + 1) * dim] = total.astype(BF)
            return 0

        lax.fori_loop(0, seq_dev // 128, body, 0)

    def take(part):
        def body(r, _):
            rows = pl.ds(mult(r * 128, 128), 128)
            ext = pl.ds(mult(SPAN * seq_dev + r * 128, 128), 128)
            for side, acc_ref in enumerate((dk, dv)):
                acc_ref[ext, :] += part[rows, side * dim : (side + 1) * dim].astype(F32)
            return 0

        lax.fori_loop(0, seq_dev // 128, body, 0)

    def fin_copy(d, side):
        o = lax.rem(me + d, HEADS)
        src = kvf.at[side, pl.ds(mult(o * tok, tok), tok), :]
        dst = (dk_hbm, dv_hbm)[side].at[:, pl.ds(mult(me * dim, dim), dim)]
        if d == 0:
            return pltpu.make_async_copy(src, dst, loc_out.at[CHUNKS + HALVES + side])
        return remote(src, dst, fin_send.at[side, d - 1], fin_recv.at[side, d - 1], seq, o)

    def keys_ready():
        @pl.when((core == 1) | (seq >= 2))
        def _():
            kv(2, 0).wait_recv()
            kv(2, 1).wait_recv()

        @pl.when(seq >= 4 - 2 * core)
        def _():
            kv(3, 0).wait_recv()
            kv(3, 1).wait_recv()

        def body(r, _):
            rows = pl.ds(mult(r * BLK, BLK), BLK)
            @pl.when(r >= missing)
            def _():
                kt[:, rows] = kx[rows, :].T
            return 0

        lax.fori_loop(0, kx.shape[0] // BLK, body, 0)

    missing = jnp.maximum(SPAN - seq, 0) * (seq_dev // BLK)
    n_kb = kx.shape[0] // BLK

    def run(f, *a):
        return functools.partial(f, *a)

    units = len(UNITS)
    early = {
        4: [run(gp0, 0)],
        6: [run(gp1, 0), run(gp0, 1)],
        7: [run(gp2, 0), run(gp1, 1)],
        8: [run(gp3, 0), run(gp2, 1)],
    }
    for u in range(units + 1):
        if u < units:
            if UNITS[u][0] == 0:
                combine(UNITS[u][1])
            first(u)
        if u >= 1:
            second(u - 1)
        if u >= 2:
            third(u - 2)
        if u == 3:
            kv_pass()
        if u == 7:
            keys_ready()
        if u >= 3:
            rest(u - 3)
            project(u - 3)
        for action in early.get(u, ()):
            action()
    project_end(0)

    def after(step, actions):
        @pl.when(step)
        def _():
            for action in actions:
                action()

    plan = {
        1: [run(third, 7), run(gp4, 0), run(gp3, 1)],
        4: [run(rest, 6), run(project, 6), run(gp0, 2), run(gp5, 0), run(gp4, 1)],
        7: [run(gp1, 2), run(gp5, 1), run(gp6, 0)],
        8: [run(rest, 7), run(project, 7), run(gp0, 3)],
        9: [run(dq_end, 0), run(project_end, 1), run(gp2, 2), run(gp6, 1)],
        10: [run(gp1, 3)],
        11: [run(gp3, 2)],
        12: [run(gp2, 3), run(gp4, 2)],
        13: [run(pack, 3), dkv_copy(0).start],
        14: [run(gp3, 3), run(gp5, 2)],
        15: [dkv_copy(0).wait_recv, run(gp4, 3)],
        17: [run(pack, 1), dkv_copy(1).start, run(gp5, 3), run(gp6, 2)],
        19: [dkv_copy(1).wait_recv],
    }

    def step(j, _):
        g = j // n_kb
        kb = lax.rem(j, n_kb)

        def variant(which, lo, n, masked):
            @pl.when((kb >= missing) & which)
            def _():
                attend(g, kb, lo, n, masked)

        variant(kb == 0, 0, half // 2, True)
        variant((kb == 1) | (kb == n_kb - 2), 0, half, True)
        variant((kb > 1) & (kb < n_kb - 2), 0, half, False)
        variant(kb == n_kb - 1, half // 2, half // 2, True)
        for when in sorted(plan):
            after(j == when, plan[when])

        @pl.when((j == 15) & (core == 1))
        def _():
            pack(4, 0)

        @pl.when((j == 15) & (core == 0))
        def _():
            pack(4)

        @pl.when((j == 15) & (seq >= 4))
        def _():
            dkv_copy(2).start()

        @pl.when((j == 15) & (core == 0))
        def _():
            pack(2, 0)

        @pl.when((j == 15) & (core == 0) & (seq >= 2))
        def _():
            dkv_copy(3).start()

        @pl.when((j == 19) & (core == 1))
        def _():
            pack(2, 1)

        @pl.when((j == 19) & (core == 1) & (seq >= 2))
        def _():
            dkv_copy(3).start()

        return 0

    lax.fori_loop(0, HALVES * n_kb, step, 0)
    dq_end(1)
    gp6(3)

    @pl.when(core == 0)
    def _():
        take(rc.at[1])

    @pl.when(seq + 4 < n_seq)
    def _():
        dkv_copy(2).wait_recv()
        take(rm2)

    @pl.when(seq + 2 < n_seq)
    def _():
        dkv_copy(3).wait_recv()
        take(rm1)

    kvf[0] = dk[last_rows, :].astype(BF)
    kvf[1] = dv[last_rows, :].astype(BF)
    for d in range(HEADS):
        fin_copy(d, 0).start()
        fin_copy(d, 1).start()

    for c in range(CHUNKS):
        for d in range(1, HEADS):
            a2a(c, d).wait_send()
        for k in range(10):
            gp_copy(c, k).wait_send()
        gp_out(c).wait()
    for u in range(units):
        whole = hid.at[pl.ds(0, 7 * sub), pl.ds(0, w)]
        remote(whole, whole, ag_send.at[u], ag_recv.at[u, 0, 0], seq, at(0, True)).wait_send()
    for which in range(2):
        @pl.when(seq + 2 < n_seq)
        def _():
            kv(0, which).wait_send()

        @pl.when(seq + 4 < n_seq)
        def _():
            kv(1, which).wait_send()

        @pl.when((core == 0) | (seq >= 2))
        def _():
            kv(2, which).wait_send()

        @pl.when(seq >= 2 + 2 * core)
        def _():
            kv(3, which).wait_send()

    dkv_copy(0).wait_send()
    dkv_copy(1).wait_send()
    @pl.when(seq >= 4)
    def _():
        dkv_copy(2).wait_send()
    @pl.when(seq >= 2)
    def _():
        dkv_copy(3).wait_send()
    for g in range(HALVES):
        dq_copy(g, 0).wait()
        for d in range(1, HEADS):
            dq_copy(g, d).wait()
    for side in range(2):
        fin_copy(0, side).wait()
        for d in range(1, HEADS):
            fin_copy(d, side).wait()


def place_kernel(*refs):
    for source, target in zip(refs[:4], refs[4:]):
        target[...] = source[...]


def local(
    out_grad, expert_rows, expert_ids, gates, out_proj, attention_output,
    saved_queries, saved_keys, saved_values, softmax_normalizer,
):
    tok, width = out_grad.shape
    n, seq_dev, dim = saved_queries.shape
    feats = n * dim
    ext = (SPAN + 1) * seq_dev
    sub = tok // HALVES
    half = HEADS * sub
    units = HALVES * CHUNKS
    w = width // CHUNKS
    ry = feats // NY
    lse = (softmax_normalizer * LOG2E).reshape(n, HEADS, HALVES, sub)
    lse = jnp.transpose(lse, (2, 0, 1, 3)).reshape(HALVES, n, half)
    anyspace = pl.BlockSpec(memory_space=pl.ANY)
    vmem = pl.BlockSpec(memory_space=pltpu.VMEM)
    dma = pltpu.SemaphoreType.DMA
    results = pl.pallas_call(
        layer_kernel,
        out_shape=[
            jax.ShapeDtypeStruct((tok, HEADS * feats), BF),
            jax.ShapeDtypeStruct((tok, HEADS * dim), BF),
            jax.ShapeDtypeStruct((tok, HEADS * dim), BF),
            jax.ShapeDtypeStruct((feats, width), BF),
        ],
        in_specs=[anyspace, vmem, vmem] + [anyspace] * 6 + [vmem],
        out_specs=[anyspace] * 4,
        scratch_shapes=[
            pltpu.VMEM(expert_rows.shape[1:], BF),
            pltpu.VMEM((HEADS * tok, width), BF),
            pltpu.VMEM(out_proj.shape, BF),
            pltpu.VMEM((HALVES, n, half, dim), BF),
            pltpu.VMEM((feats, seq_dev), BF),
            pltpu.VMEM((tok, width), BF),
            pltpu.VMEM((2, tok, expert_rows.shape[1]), BF),
            pltpu.VMEM((HALVES, half, feats), F32),
            pltpu.VMEM((HALVES, half, feats), BF),
            pltpu.VMEM((HALVES, n, half), F32),
            pltpu.VMEM((HALVES, n, half, dim), BF),
            pltpu.VMEM((ext, dim), BF),
            pltpu.VMEM((ext, dim), BF),
            pltpu.VMEM((dim, ext), BF),
            pltpu.VMEM((ext, dim), F32),
            pltpu.VMEM((ext, dim), F32),
            pltpu.VMEM((n, dim, half), F32),
            pltpu.VMEM((HALVES, half, feats), BF),
            pltpu.VMEM((CHUNKS, feats, w // 2), BF),
            pltpu.VMEM((CHUNKS, 3, ry, w // 2), BF),
            pltpu.VMEM((CHUNKS, ry, w // 2), F32),
            pltpu.VMEM((CHUNKS, ry // 2, w // 2), BF),
            pltpu.VMEM((CHUNKS, ry // 2, w // 2), BF),
            pltpu.VMEM((feats, width), BF),
            pltpu.VMEM((SPAN, seq_dev, 2 * dim), BF),
            pltpu.VMEM((2, seq_dev, 2 * dim), BF),
            pltpu.VMEM((seq_dev, 2 * dim), BF),
            pltpu.VMEM((seq_dev, 2 * dim), BF),
            pltpu.VMEM((2, seq_dev, dim), BF),
            dma((CHUNKS, HEADS - 1)), dma((CHUNKS, HEADS - 1)),
            dma((units,)), dma((units, 4, HEADS)),
            dma((SPAN, 2)), dma((SPAN, 2)),
            dma((CHUNKS, 10)), dma((CHUNKS, 10)),
            dma((HALVES, HEADS - 1)), dma((HALVES, HEADS - 1)),
            dma((4,)), dma((4,)),
            dma((2, HEADS - 1)), dma((2, HEADS - 1)),
            dma((5,)), dma((2, HALVES, HEADS)), dma((CHUNKS + HALVES + 2,)),
        ],
        compiler_params=pltpu.CompilerParams(
            collective_id=0, has_side_effects=True, vmem_limit_bytes=62 * 2**20
        ),
        cost_estimate=pl.CostEstimate(flops=3 * 10**10, bytes_accessed=60 * 2**20, transcendentals=10**7),
        name="layer_backward",
    )(
        expert_rows[0], expert_ids.T, gates.T, out_grad, out_proj, attention_output,
        saved_queries, saved_keys[0], saved_values[0], lse,
    )
    steps = 8
    slabs = [pl.BlockSpec((r.shape[0] // steps, r.shape[1]), lambda i: (i, 0)) for r in results]
    return pl.pallas_call(
        place_kernel,
        grid=(steps,),
        out_shape=[jax.ShapeDtypeStruct(r.shape, r.dtype) for r in results],
        in_specs=slabs,
        out_specs=slabs,
        name="place_results",
    )(*results)


def solution(mesh):
    tokens = P(("seq", "head"), None)
    by_head = P("head", "seq", None)
    return jax.shard_map(
        local,
        mesh=mesh,
        in_specs=(tokens, by_head, tokens, tokens, P("head", None)) + (by_head,) * 4 + (P("head", "seq"),),
        out_specs=(tokens, tokens, tokens, P("head", None)),
        check_vma=False,
    )
```

time: 768 us -> 284 us (0.37); the launches traced: 757 us -> 284 us
  waiting for transfers between devices: 309 us -> 0 us
  Pallas kernels: 0 us -> 281 us
  blocking collectives: 126 us -> 0 us
  matrix products: 115 us -> 0 us
  local copies, waits for them, and re-layouts: 97.2 us -> 0.79 us
  other arithmetic: 51.5 us -> 0.72 us
  starting transfers between devices: 42.4 us -> 0 us
  between operations: 14.7 us -> 0.65 us
    pallas_call x0 -> x2, Pallas kernels: none -> 281 us  [the longest x1 274 us: local(): pl.pallas_call(layer_kernel, out_shape=[jax.ShapeDtypeStruct((tok, HEADS...]
    ppermute x8 -> x0, waiting for transfers between devices: 130 us -> none  [shifted(): return lax.ppermute(block, axis, route)]
    psum x1 -> x0, blocking collectives: 126 us -> none  [local(): summed_proj = lax.psum(partial_value, 'seq')]
    dot_general x32 -> x0, matrix products: 115 us -> none  [the longest x6 25.6 us: block_step(): lax.dot_general(query_blk, key_blk, (((1,), (1,)), ((), ())), preferred_e...]
    all_gather x1 -> x0, waiting for transfers between devices: 109 us -> none  [local(): piece = lax.all_gather(hidden, 'head', axis=0, tiled=True)]
    all_to_all x4 -> x0, waiting for transfers between devices: 69.8 us -> none  [the longest x1 69.8 us: local(): lax.all_to_all(expert_rows, 'head', split_axis=1, concat_axis=0, tiled=True)]
    unnamed x31 -> x0, local copies, waits for them, and re-layouts: 55.6 us -> none
    unnamed x1 -> x0, other arithmetic: 38.9 us -> none
  transfers between devices with their start and end apart: 13 -> 0, of which waited for: 8 -> 0; matrix products, arithmetic and copies ran while one was open for 4% -> 0% of each run, Pallas kernels for 0% -> 0%
where the time goes in v2:
time: 284 us
  Pallas kernels  281 us (99%)
    pallas_call x1, Pallas kernels, local(): pl.pallas_call(layer_kernel, out_shape=[jax.ShapeDtypeStruct((tok, HEADS...  274 us
    pallas_call x1, Pallas kernels, local(): pl.pallas_call(place_kernel, grid=(steps,), out_shape=[jax.ShapeDtypeStru...  7.76 us

profile of v2, /device:TPU:24, one launch (start us, length us, event | category | flops | bytes accessed | tf_op | source)
XLA Modules:
  0.0 283.6 jit_solution(7895060721843447791)
XLA Ops:
  0.6 0.7 broadcast_multiply_fusion
  1.4 0.1 reshape.14
  1.5 0.1 reshape.15
  1.5 0.6 copy.16.lse_ref
  2.2 273.6 %layer_backward.1 = (bf16[128,3072]{1,0:T(8,128)(2,1)}, bf16[128,1024]{1,0:T(8,128)(2,1)}, bf16[128,1024]{1,0:T(8,128)(2,1)}, bf16[384,6144]{1,0:T(8,128)(2,1)}) custom-call(bf16[512,6144]{1,0:T(8,128)(2,1)} %bitcast.13, s32[2,128]{1,0:T(2,128)} %bitcast.16, f32[2,128]{1,0:T(2,128)} %bitcast.17, bf16[128,6144]{1,0:T(8,128)(2,1)} %resid_hbm.1, ...), custom_call_target="tpu_custom_call" | custom-call | flops 30000001024 | bytes 62914560 | tf_op jit(solution)/shard_map/layer_backward/pallas_call | solution.py:658
  275.8 7.8 %place_results.1 = (bf16[128,3072]{1,0:T(8,128)(2,1)}, bf16[128,1024]{1,0:T(8,128)(2,1)}, bf16[128,1024]{1,0:T(8,128)(2,1)}, bf16[384,6144]{1,0:T(8,128)(2,1)}) custom-call(bf16[128,3072]{1,0:T(8,128)(2,1)} %get-tuple-element.8.refs_0_, bf16[128,1024]{1,0:T(8,128)(2,1)} %get-tuple-element.9.refs_1_, bf16[128,1024]{1,0:T(8,128)(2,1)} %get-tuple-element.10.refs_2_, ...), custom_call_target="tpu_custom_call" | custom-call | tf_op jit(solution)/shard_map/place_results/pallas_call | solution.py:718
  (1 shorter events, 0.0 us)

commit v3 on v2

--- a/solution.py
+++ b/solution.py
@@ -21,7 +21,7 @@
 HALVES = 2
 SPAN = 4
 BLK = 512
-UNITS = ((0, 0), (1, 0), (0, 1), (1, 1), (0, 2), (0, 3), (1, 2), (1, 3))
+UNITS = ((0, 0), (1, 0), (0, 1), (1, 1), (0, 2), (1, 2), (0, 3), (1, 3))
 
 
 def layer_kernel(
@@ -44,7 +44,6 @@
     half = HEADS * sub
     cap = recv.shape[0] // HEADS
     w = width // CHUNKS
-    cuts = (0, w // 3, 2 * w // 3, 5 * w // 6, w)
     wh = w // 2
     n_heads = attn.shape[1]
     dim = 128
@@ -183,60 +182,52 @@
         for h in range(n_heads):
             attn_t[h * dim : (h + 1) * dim, g * half : (g + 1) * half] = attn[g, h].T
 
-    def block(u, p, o):
+    cuts = (0, w // 6, w // 2, 5 * w // 6, w)
+    everything, x_first, forward, backward = (0, 4), (1, 3), (0, 2), (2, 4)
+    quarter = ((0, 1), (1, 2), (2, 3), (3, 4))
+
+    def send(u, o, part, sem, dz, flip):
         g, c = UNITS[u]
-        return hid.at[pl.ds(mult(g * half + o * sub, sub), sub), pl.ds(c * w + cuts[p], cuts[p + 1] - cuts[p])]
-
-    def send(u, p, o, dz, flip):
-        return remote(block(u, p, o), block(u, p, o), ag_send.at[u], ag_recv.at[u, p, o], seq, at(dz, flip))
-
-    def arrived(u, p, o):
-        send(u, p, o, 0, True).wait_recv()
-
-    def ways(p):
-        return (3, 1) if p % 2 == 0 else (1, 3)
+        lo, hi = cuts[part[0]], cuts[part[1]]
+        block = hid.at[pl.ds(mult(g * half + o * sub, sub), sub), pl.ds(c * w + lo, hi - lo)]
+        return remote(block, block, ag_send.at[u], ag_recv.at[u, o, sem], seq, at(dz, flip))
+
+    def arrived(u, o, part, sem):
+        send(u, o, part, sem, 0, True).wait_recv()
 
     def first(u):
-        for p in range(4):
-            send(u, p, me, 0, True).start()
-            send(u, p, me, 1, False).start()
-            send(u, p, me, 3, False).start()
+        send(u, me, everything, 0, 0, True).start()
+        send(u, me, everything, 0, 1, False).start()
+        send(u, me, everything, 0, 3, False).start()
 
     def second(u):
-        for p in range(4):
-            back, on = ways(p)
-            arrived(u, p, at(back, False))
-            send(u, p, at(back, False), on, False).start()
-            if p < 2:
-                arrived(u, p, at(0, True))
-                send(u, p, at(0, True), 1, False).start()
-                send(u, p, at(0, True), 3, False).start()
-            else:
-                send(u, p, at(back, False), 0, True).start()
-                arrived(u, p, at(on, False))
-                send(u, p, at(on, False), 0, True).start()
+        arrived(u, at(3, False), everything, 0)
+        send(u, at(3, False), forward, 0, 1, False).start()
+        arrived(u, at(0, True), everything, 0)
+        send(u, at(0, True), x_first, 0, 3, False).start()
+        send(u, at(0, True), x_first, 0, 1, False).start()
+        arrived(u, at(1, False), everything, 0)
+        send(u, at(1, False), backward, 1, 3, False).start()
+        for dz in (3, 1):
+            send(u, at(dz, False), quarter[0], 1, 0, True).start()
+            send(u, at(dz, False), quarter[3], 2, 0, True).start()
 
     def third(u):
-        for p in range(4):
-            back, on = ways(p)
-            if p < 2:
-                arrived(u, p, at(back, True))
-                send(u, p, at(back, True), on, False).start()
-            else:
-                arrived(u, p, at(2, False))
-                send(u, p, at(2, False), 0, True).start()
+        arrived(u, at(3, True), x_first, 0)
+        send(u, at(3, True), quarter[1], 0, 1, False).start()
+        arrived(u, at(1, True), x_first, 0)
+        send(u, at(1, True), quarter[2], 3, 3, False).start()
+        arrived(u, at(2, False), forward, 0)
+        send(u, at(2, False), quarter[0], 1, 0, True).start()
+        arrived(u, at(2, False), backward, 1)
+        send(u, at(2, False), quarter[3], 2, 0, True).start()
 
     def rest(u):
-        for p in range(4):
-            back, on = ways(p)
-            if p < 2:
-                arrived(u, p, at(on, False))
-                arrived(u, p, at(2, False))
-                arrived(u, p, at(on, True))
-                arrived(u, p, at(2, True))
-            else:
-                for dz in range(NZ):
-                    arrived(u, p, at(dz, True))
+        for dz in (1, 2, 3):
+            arrived(u, at(dz, True), quarter[0], 1)
+            arrived(u, at(dz, True), quarter[3], 2)
+        arrived(u, at(2, True), quarter[1], 0)
+        arrived(u, at(2, True), quarter[2], 3)
 
     def combine(c):
         for d in range(1, HEADS):
@@ -472,16 +463,18 @@
     units = len(UNITS)
     early = {
         4: [run(gp0, 0)],
-        6: [run(gp1, 0), run(gp0, 1)],
-        7: [run(gp2, 0), run(gp1, 1)],
-        8: [run(gp3, 0), run(gp2, 1)],
+        5: [run(gp1, 0)],
+        6: [run(gp2, 0), run(gp0, 1)],
+        7: [run(gp3, 0), run(gp1, 1)],
+        8: [run(gp4, 0), run(gp2, 1), run(gp0, 2)],
+        9: [run(gp5, 0), run(gp3, 1), run(gp1, 2)],
     }
-    for u in range(units + 1):
+    for u in range(units + 2):
         if u < units:
             if UNITS[u][0] == 0:
                 combine(UNITS[u][1])
             first(u)
-        if u >= 1:
+        if 1 <= u <= units:
             second(u - 1)
         if u >= 2:
             third(u - 2)
@@ -503,24 +496,25 @@
                 action()
 
     plan = {
-        1: [run(third, 7), run(gp4, 0), run(gp3, 1)],
-        4: [run(rest, 6), run(project, 6), run(gp0, 2), run(gp5, 0), run(gp4, 1)],
-        7: [run(gp1, 2), run(gp5, 1), run(gp6, 0)],
-        8: [run(rest, 7), run(project, 7), run(gp0, 3)],
-        9: [run(dq_end, 0), run(project_end, 1), run(gp2, 2), run(gp6, 1)],
-        10: [run(gp1, 3)],
-        11: [run(gp3, 2)],
-        12: [run(gp2, 3), run(gp4, 2)],
+        1: [run(gp6, 0), run(gp4, 1), run(gp2, 2)],
+        3: [run(rest, 7), run(gp0, 3), run(project, 7)],
+        4: [run(gp5, 1), run(gp3, 2)],
+        5: [run(gp1, 3)],
+        6: [run(gp6, 1), run(gp4, 2)],
+        8: [run(gp2, 3)],
+        9: [run(dq_end, 0), run(project_end, 1), run(gp5, 2)],
+        10: [run(gp3, 3)],
+        12: [run(gp6, 2), run(gp4, 3)],
         13: [run(pack, 3), dkv_copy(0).start],
-        14: [run(gp3, 3), run(gp5, 2)],
-        15: [dkv_copy(0).wait_recv, run(gp4, 3)],
-        17: [run(pack, 1), dkv_copy(1).start, run(gp5, 3), run(gp6, 2)],
-        19: [dkv_copy(1).wait_recv],
+        15: [run(pack, 1), dkv_copy(1).start, run(gp5, 3), dkv_copy(0).wait_recv],
+        17: [dkv_copy(1).wait_recv],
+        18: [run(gp6, 3)],
     }
 
     def step(j, _):
         g = j // n_kb
-        kb = lax.rem(j, n_kb)
+        turn = lax.rem(j, n_kb)
+        kb = turn + jnp.where((turn == 4) | (turn == 5), 2, jnp.where((turn == 6) | (turn == 7), -2, 0))
 
         def variant(which, lo, n, masked):
             @pl.when((kb >= missing) & which)
@@ -546,19 +540,15 @@
         def _():
             dkv_copy(2).start()
 
-        @pl.when((j == 15) & (core == 0))
+        @pl.when((j == 17) & (core == 0))
         def _():
             pack(2, 0)
 
-        @pl.when((j == 15) & (core == 0) & (seq >= 2))
-        def _():
-            dkv_copy(3).start()
-
-        @pl.when((j == 19) & (core == 1))
+        @pl.when((j == 17) & (core == 1))
         def _():
             pack(2, 1)
 
-        @pl.when((j == 19) & (core == 1) & (seq >= 2))
+        @pl.when((j == 17) & (seq >= 2))
         def _():
             dkv_copy(3).start()
 
@@ -566,7 +556,6 @@
 
     lax.fori_loop(0, HALVES * n_kb, step, 0)
     dq_end(1)
-    gp6(3)
 
     @pl.when(core == 0)
     def _():
@@ -632,9 +621,26 @@
             fin_copy(d, side).wait()
 
 
+PLACES = tuple((3, i, 6) for i in range(6)) + tuple((0, i, 2) for i in range(2)) + ((1, 0, 1), (2, 0, 1))
+
+
 def place_kernel(*refs):
-    for source, target in zip(refs[:4], refs[4:]):
-        target[...] = source[...]
+    sources, targets, held, sems = refs[:4], refs[4:8], refs[8:12], refs[12]
+    copies = []
+    for i, (which, part, parts) in enumerate(PLACES):
+        n = sources[which].shape[0] // parts
+        rows = pl.ds(part * n, n)
+        copies.append([
+            pltpu.make_async_copy(sources[which].at[rows, :], held[which].at[rows, :], sems.at[0, i]),
+            pltpu.make_async_copy(held[which].at[rows, :], targets[which].at[rows, :], sems.at[1, i]),
+        ])
+    for come, _ in copies:
+        come.start()
+    for come, go in copies:
+        come.wait()
+        go.start()
+    for _, go in copies:
+        go.wait()
 
 
 def local(
@@ -696,7 +702,7 @@
             pltpu.VMEM((seq_dev, 2 * dim), BF),
             pltpu.VMEM((2, seq_dev, dim), BF),
             dma((CHUNKS, HEADS - 1)), dma((CHUNKS, HEADS - 1)),
-            dma((units,)), dma((units, 4, HEADS)),
+            dma((units,)), dma((units, HEADS, 4)),
             dma((SPAN, 2)), dma((SPAN, 2)),
             dma((CHUNKS, 10)), dma((CHUNKS, 10)),
             dma((HALVES, HEADS - 1)), dma((HALVES, HEADS - 1)),
@@ -713,14 +719,13 @@
         expert_rows[0], expert_ids.T, gates.T, out_grad, out_proj, attention_output,
         saved_queries, saved_keys[0], saved_values[0], lse,
     )
-    steps = 8
-    slabs = [pl.BlockSpec((r.shape[0] // steps, r.shape[1]), lambda i: (i, 0)) for r in results]
     return pl.pallas_call(
         place_kernel,
-        grid=(steps,),
         out_shape=[jax.ShapeDtypeStruct(r.shape, r.dtype) for r in results],
-        in_specs=slabs,
-        out_specs=slabs,
+        in_specs=[anyspace] * 4,
+        out_specs=[anyspace] * 4,
+        scratch_shapes=[pltpu.VMEM(r.shape, r.dtype) for r in results] + [dma((2, len(PLACES)))],
+        compiler_params=pltpu.CompilerParams(vmem_limit_bytes=62 * 2**20),
         name="place_results",
     )(*results)
 

time: 284 us -> 277 us (0.975)
  Pallas kernels: 281 us -> 274 us
    pallas_call x1, Pallas kernels: 274 us -> 269 us  [local(): pl.pallas_call(layer_kernel, out_shape=[jax.ShapeDtypeStruct((tok, HEADS...]
where the time goes in v3:
time: 277 us
  Pallas kernels  274 us (99%)
    pallas_call x1, Pallas kernels, local(): pl.pallas_call(layer_kernel, out_shape=[jax.ShapeDtypeStruct((tok, HEADS...  269 us

profile of v3, /device:TPU:24, one launch (start us, length us, event | category | flops | bytes accessed | tf_op | source)
XLA Modules:
  0.0 276.6 jit_solution(9985026093650030754)
XLA Ops:
  0.6 0.7 broadcast_multiply_fusion
  1.4 0.1 reshape.14
  1.5 0.1 reshape.15
  1.5 0.6 copy.16.lse_ref
  2.2 269.1 %layer_backward.1 = (bf16[128,3072]{1,0:T(8,128)(2,1)}, bf16[128,1024]{1,0:T(8,128)(2,1)}, bf16[128,1024]{1,0:T(8,128)(2,1)}, bf16[384,6144]{1,0:T(8,128)(2,1)}) custom-call(bf16[512,6144]{1,0:T(8,128)(2,1)} %bitcast.13, s32[2,128]{1,0:T(2,128)} %bitcast.16, f32[2,128]{1,0:T(2,128)} %bitcast.17, bf16[128,6144]{1,0:T(8,128)(2,1)} %resid_hbm.1, ...), custom_call_target="tpu_custom_call" | custom-call | flops 30000001024 | bytes 62914560 | tf_op jit(solution)/shard_map/layer_backward/pallas_call | solution.py:664
  271.3 5.2 %place_results.1 = (bf16[128,3072]{1,0:T(8,128)(2,1)}, bf16[128,1024]{1,0:T(8,128)(2,1)}, bf16[128,1024]{1,0:T(8,128)(2,1)}, bf16[384,6144]{1,0:T(8,128)(2,1)}) custom-call(bf16[128,3072]{1,0:T(8,128)(2,1)} %get-tuple-element.8.refs_0_, bf16[128,1024]{1,0:T(8,128)(2,1)} %get-tuple-element.9.refs_1_, bf16[128,1024]{1,0:T(8,128)(2,1)} %get-tuple-element.10.refs_2_, ...), custom_call_target="tpu_custom_call" | custom-call | tf_op jit(solution)/shard_map/place_results/pallas_call | solution.py:722
  (1 shorter events, 0.0 us)

commit v4 on v3

--- a/solution.py
+++ b/solution.py
@@ -182,12 +182,13 @@
         for h in range(n_heads):
             attn_t[h * dim : (h + 1) * dim, g * half : (g + 1) * half] = attn[g, h].T
 
-    cuts = (0, w // 6, w // 2, 5 * w // 6, w)
+    cuts_of = ((0, w // 12, w // 2, 5 * w // 6, w), (0, w // 6, w // 2, 11 * w // 12, w))
     everything, x_first, forward, backward = (0, 4), (1, 3), (0, 2), (2, 4)
     quarter = ((0, 1), (1, 2), (2, 3), (3, 4))
 
     def send(u, o, part, sem, dz, flip):
         g, c = UNITS[u]
+        cuts = cuts_of[u % 2]
         lo, hi = cuts[part[0]], cuts[part[1]]
         block = hid.at[pl.ds(mult(g * half + o * sub, sub), sub), pl.ds(c * w + lo, hi - lo)]
         return remote(block, block, ag_send.at[u], ag_recv.at[u, o, sem], seq, at(dz, flip))

time: 277 us -> 280 us (1.011)
  Pallas kernels: 274 us -> 277 us
    pallas_call x1, Pallas kernels: 269 us -> 272 us  [local(): pl.pallas_call(layer_kernel, out_shape=[jax.ShapeDtypeStruct((tok, HEADS...]
where the time goes in v4:
time: 280 us
  Pallas kernels  277 us (99%)
    pallas_call x1, Pallas kernels, local(): pl.pallas_call(layer_kernel, out_shape=[jax.ShapeDtypeStruct((tok, HEADS...  272 us

profile of v4, /device:TPU:24, one launch (start us, length us, event | category | flops | bytes accessed | tf_op | source)
XLA Modules:
  0.0 279.5 jit_solution(15237761567145412034)
XLA Ops:
  0.6 0.7 broadcast_multiply_fusion
  1.4 0.1 reshape.14
  1.5 0.1 reshape.15
  1.5 0.6 copy.16.lse_ref
  2.2 272.0 %layer_backward.1 = (bf16[128,3072]{1,0:T(8,128)(2,1)}, bf16[128,1024]{1,0:T(8,128)(2,1)}, bf16[128,1024]{1,0:T(8,128)(2,1)}, bf16[384,6144]{1,0:T(8,128)(2,1)}) custom-call(bf16[512,6144]{1,0:T(8,128)(2,1)} %bitcast.13, s32[2,128]{1,0:T(2,128)} %bitcast.16, f32[2,128]{1,0:T(2,128)} %bitcast.17, bf16[128,6144]{1,0:T(8,128)(2,1)} %resid_hbm.1, ...), custom_call_target="tpu_custom_call" | custom-call | flops 30000001024 | bytes 62914560 | tf_op jit(solution)/shard_map/layer_backward/pallas_call | solution.py:665
  274.2 5.2 %place_results.1 = (bf16[128,3072]{1,0:T(8,128)(2,1)}, bf16[128,1024]{1,0:T(8,128)(2,1)}, bf16[128,1024]{1,0:T(8,128)(2,1)}, bf16[384,6144]{1,0:T(8,128)(2,1)}) custom-call(bf16[128,3072]{1,0:T(8,128)(2,1)} %get-tuple-element.8.refs_0_, bf16[128,1024]{1,0:T(8,128)(2,1)} %get-tuple-element.9.refs_1_, bf16[128,1024]{1,0:T(8,128)(2,1)} %get-tuple-element.10.refs_2_, ...), custom_call_target="tpu_custom_call" | custom-call | tf_op jit(solution)/shard_map/place_results/pallas_call | solution.py:723
  (1 shorter events, 0.0 us)

commit v5 on v4

--- a/solution.py
+++ b/solution.py
@@ -182,7 +182,7 @@
         for h in range(n_heads):
             attn_t[h * dim : (h + 1) * dim, g * half : (g + 1) * half] = attn[g, h].T
 
-    cuts_of = ((0, w // 12, w // 2, 5 * w // 6, w), (0, w // 6, w // 2, 11 * w // 12, w))
+    cuts_of = ((0, w // 6, w // 2, 3 * w // 4, w), (0, w // 4, w // 2, 5 * w // 6, w))
     everything, x_first, forward, backward = (0, 4), (1, 3), (0, 2), (2, 4)
     quarter = ((0, 1), (1, 2), (2, 3), (3, 4))
 

time: 280 us -> 272 us (0.971)
  Pallas kernels: 277 us -> 269 us
    pallas_call x1, Pallas kernels: 272 us -> 264 us  [local(): pl.pallas_call(layer_kernel, out_shape=[jax.ShapeDtypeStruct((tok, HEADS...]
where the time goes in v5:
time: 272 us; the launch traced here: 271 us
  Pallas kernels  269 us (99%)
    pallas_call x1, Pallas kernels, local(): pl.pallas_call(layer_kernel, out_shape=[jax.ShapeDtypeStruct((tok, HEADS...  264 us

profile of v5, /device:TPU:24, one launch (start us, length us, event | category | flops | bytes accessed | tf_op | source)
XLA Modules:
  0.0 271.3 jit_solution(9665086782135692890)
XLA Ops:
  0.6 0.7 broadcast_multiply_fusion
  1.4 0.1 reshape.14
  1.5 0.1 reshape.15
  1.5 0.6 copy.16.lse_ref
  2.2 263.8 %layer_backward.1 = (bf16[128,3072]{1,0:T(8,128)(2,1)}, bf16[128,1024]{1,0:T(8,128)(2,1)}, bf16[128,1024]{1,0:T(8,128)(2,1)}, bf16[384,6144]{1,0:T(8,128)(2,1)}) custom-call(bf16[512,6144]{1,0:T(8,128)(2,1)} %bitcast.13, s32[2,128]{1,0:T(2,128)} %bitcast.16, f32[2,128]{1,0:T(2,128)} %bitcast.17, bf16[128,6144]{1,0:T(8,128)(2,1)} %resid_hbm.1, ...), custom_call_target="tpu_custom_call" | custom-call | flops 30000001024 | bytes 62914560 | tf_op jit(solution)/shard_map/layer_backward/pallas_call | solution.py:665
  266.0 5.2 %place_results.1 = (bf16[128,3072]{1,0:T(8,128)(2,1)}, bf16[128,1024]{1,0:T(8,128)(2,1)}, bf16[128,1024]{1,0:T(8,128)(2,1)}, bf16[384,6144]{1,0:T(8,128)(2,1)}) custom-call(bf16[128,3072]{1,0:T(8,128)(2,1)} %get-tuple-element.8.refs_0_, bf16[128,1024]{1,0:T(8,128)(2,1)} %get-tuple-element.9.refs_1_, bf16[128,1024]{1,0:T(8,128)(2,1)} %get-tuple-element.10.refs_2_, ...), custom_call_target="tpu_custom_call" | custom-call | tf_op jit(solution)/shard_map/place_results/pallas_call | solution.py:723
  (1 shorter events, 0.0 us)
